TPU v7x, 128 devices: a whole 4x4x4 slice. The times are simulated.
128 devices in a mesh: dp: 16 (over z_lo, x, core), mp: 8 (over y, z_hi).
Axes of the slice: x: 4, y: 4, z: 4 (z_hi: 2, z_lo: 2; z = z_hi * 2 + z_lo), core: 2. Of those that a mesh axis runs over, the one named last changes fastest.
Arguments:
- hidden: bfloat16 [8192, 4096], P('dp'), may hold values from -6 to 6
- segment_ids: int32 [16, 512], P('dp'), may hold values from 0 to 15, never falling along the last dimension, each value on 1 to 128 neighbouring positions
- attn_gain: float32 [4096], replicated, may hold values from 0.25 to 1.75
- w_query: bfloat16 [4096, 4096], P(None, 'mp'), as said below
- w_key: bfloat16 [4096, 1024], P(None, 'mp'), as said below
- w_value: bfloat16 [4096, 1024], P(None, 'mp'), may hold values from -0.09375 to 0.09375
- w_out: bfloat16 [4096, 4096], P('mp'), may hold values from -0.09375 to 0.09375
- final_gain: float32 [4096], replicated, may hold values from 0.25 to 1.75
- adapter: bfloat16 [4096, 1024], replicated, may hold values from -0.09375 to 0.09375
- features: bfloat16 [256, 1024], P(('dp', 'mp')), may hold values from -6 to 6
- ln_gain: float32 [1024], replicated, may hold values from 0.25 to 1.75
- ln_bias: float32 [1024], replicated, may hold values from -3 to 3
- pair_ids: int32 [256], replicated, may hold values from 0 to 255, each once
Outputs:
- loss: float32 [], replicated
- adapter_grad: float32 [4096, 1024], P(('dp', 'mp'))
- feature_grad: float32 [256, 1024], P(('dp', 'mp'))
Inputs may be any that keep to these rules, and one draw needn't show every extreme that they name: `segment_ids`: within each row segment ids never fall; each of the 16 ids has 1 to 128 tokens and one has exactly 128. `pair_ids`: each text is paired with exactly one image. `w_query`: independent entries of mean zero and deviation about 4096^(-1/2). `w_key`: entries of mean zero.
All inputs are finite; a program needn't handle non-finite values.
Results may differ from a plain program's by a relative error of at most 0.02.
Values may be sent and summed in bfloat16 or wider, within the bound.
No kernel may reach another device: no remote copies, remote signals or barrier semaphores. Data moves between devices by JAX's collectives and lax.ppermute only.
A program may use at most 128 MiB of HBM per device.

v0:
```python
import jax
import jax.numpy as jnp
import numpy as np
from jax import lax
from jax.experimental import pallas as pl
from jax.experimental.pallas import tpu as pltpu
from jax.sharding import PartitionSpec as P

HD = 128
DOCS_DEV = 16
SCALE = 1.0 / 0.07
EPS = 1e-05
HIGH = lax.Precision.HIGHEST
F32 = jnp.float32
BF16 = jnp.bfloat16


def rope_tables(length):
    half = HD // 2
    freq = 500000.0 ** (-np.arange(half) * 2.0 / HD)
    angle = np.arange(length)[:, None] * freq[None, :]
    cosine = np.concatenate([np.cos(angle), np.cos(angle)], axis=1)
    sine = np.concatenate([-np.sin(angle), np.sin(angle)], axis=1)
    return cosine.astype(np.float32), sine.astype(np.float32)


def dot(left, right, precision=None):
    return jnp.dot(left, right, precision=precision, preferred_element_type=F32)


def dot_rows(left, right, precision=None):
    return lax.dot_general(
        left, right, (((1,), (1,)), ((), ())), precision=precision, preferred_element_type=F32
    )


def text_kernel(
    hidden, w_query, w_key, w_value, w_out, gain, cosine, sine, seg,
    z_send, up_1, down_1, ordered_out,
    hid, w_in, w_up, table, acc, query, keys, values, att, ordered, stage, stage_send, sems, out_sems,
):
    length, width = hidden.shape
    q_local = w_query.shape[1] // HD
    parts = 4
    span = width // parts
    q_cols = w_query.shape[1]
    kv_cols = w_key.shape[1]
    copies = []
    for part in range(parts):
        rows = pl.ds(part * span, span)
        group = [
            pltpu.make_async_copy(hidden.at[:, rows], hid.at[:, rows], sems.at[part, 0]),
            pltpu.make_async_copy(
                w_query.at[rows, :], w_in.at[rows, pl.ds(0, q_cols)], sems.at[part, 1]
            ),
            pltpu.make_async_copy(
                w_key.at[rows, :], w_in.at[rows, pl.ds(q_cols, kv_cols)], sems.at[part, 2]
            ),
            pltpu.make_async_copy(
                w_value.at[rows, :], w_in.at[rows, pl.ds(q_cols + kv_cols, kv_cols)], sems.at[part, 3]
            ),
        ]
        for copy in group:
            copy.start()
        copies.append(group)
    table_copies = [
        pltpu.make_async_copy(cosine, table.at[0], sems.at[parts, 1]),
        pltpu.make_async_copy(sine, table.at[1], sems.at[parts, 2]),
    ]
    for copy in table_copies:
        copy.start()
    up_copy = pltpu.make_async_copy(w_out, w_up, sems.at[parts, 0])
    up_copy.start()
    squares = jnp.zeros((length, HD), F32)
    for part in range(parts):
        for copy in copies[part]:
            copy.wait()
        cols = slice(part * span, (part + 1) * span)
        stream = hid[:, cols].astype(F32)
        for lane in range(0, span, HD):
            piece = stream[:, lane : lane + HD]
            squares = squares + piece * piece
        scaled = (stream * gain[:, cols]).astype(BF16)
        product = dot(scaled, w_in[cols, :])
        if part == 0:
            acc[...] = product
        else:
            acc[...] += product
    norm = lax.rsqrt(jnp.sum(squares, axis=1, keepdims=True) * (1.0 / width) + EPS)
    for copy in table_copies:
        copy.wait()
    cos_t = table[0] * norm
    sin_t = table[1] * norm
    value = acc[:, q_cols : q_cols + HD]
    keys[...] = (value * cos_t + pltpu.roll(value, HD // 2, 1) * sin_t).astype(BF16)
    values[:, 0:HD] = (acc[:, q_cols + HD :] * norm).astype(BF16)
    values[:, HD:] = jnp.ones((length, HD), BF16)
    cos_t = cos_t * HD ** (-0.5)
    sin_t = sin_t * HD ** (-0.5)
    for head in range(q_local):
        lanes = slice(head * HD, (head + 1) * HD)
        value = acc[:, lanes]
        query[:, lanes] = (value * cos_t + pltpu.roll(value, HD // 2, 1) * sin_t).astype(BF16)
    block = 128
    seg_f = seg[...].astype(F32)
    for at in range(length // block):
        first = max(0, at - 1) * block
        last = (at + 1) * block
        rows = slice(at * block, last)
        seg_q = jnp.broadcast_to(seg_f[:, rows], (block, block)).T
        masks = []
        for key_at in range(first, last, block):
            seg_k = jnp.broadcast_to(seg_f[:, key_at : key_at + block], (block, block))
            live = seg_q == seg_k
            if key_at == at * block:
                live = live & (
                    lax.broadcasted_iota(jnp.int32, (block, block), 0)
                    >= lax.broadcasted_iota(jnp.int32, (block, block), 1)
                )
            masks.append(jnp.where(live, 0.0, -1e30))
        mask = masks[0] if len(masks) == 1 else jnp.concatenate(masks, axis=1)
        mask = jnp.concatenate([mask] * q_local, axis=0)
        stacked = jnp.concatenate(
            [query[rows, head * HD : (head + 1) * HD] for head in range(q_local)], axis=0
        )
        score = dot_rows(stacked, keys[first:last, :]) + mask
        weight = jnp.exp(score - jnp.max(score, axis=1, keepdims=True)).astype(BF16)
        result = dot(weight, values[first:last, :])
        result = (result[:, 0:HD] / result[:, HD:]).astype(BF16)
        for head in range(q_local):
            att[rows, head * HD : (head + 1) * HD] = result[head * block : (head + 1) * block]
    index = lax.axis_index("mp")
    y, z = index // 2, lax.rem(index, 2)
    small = length // 8
    for step in range(4):
        base = lax.rem(y + step, 4) * 2
        mine = pl.multiple_of((base + z) * small, small)
        other = pl.multiple_of((base + 1 - z) * small, small)
        at = step * small
        ordered[pl.ds(at, small), :] = att[pl.ds(mine, small), :]
        ordered[pl.ds(4 * small + at, small), :] = att[pl.ds(other, small), :]
    up_copy.wait()
    side = up_1.shape[1]
    cut = 2 * side
    sends = []

    def ship(source, target):
        send = pltpu.make_async_copy(source, target, out_sems.at[len(sends)])
        send.start()
        sends.append(send)

    for start, stop in pieces(cut, width):
        stage_send[:, start - cut : stop - cut] = dot(
            ordered[4 * small :, :], w_up[:, start:stop]
        ).astype(BF16)
    ship(stage_send, z_send)
    ship(ordered, ordered_out)
    far = jnp.concatenate(
        [ordered[2 * small : 3 * small, :], ordered[6 * small : 7 * small, :]], axis=0
    )
    for start, stop in pieces(0, cut):
        stage[:, start:stop] = dot(far, w_up[:, start:stop]).astype(BF16)
    ship(stage.at[:, pl.ds(0, side)], up_1)
    ship(stage.at[:, pl.ds(side, side)], down_1)
    for send in sends:
        send.wait()


def pieces(first, last, chunk=512):
    edges = list(range(first, last - chunk + 1, chunk)) + [last]
    return list(zip(edges[:-1], edges[1:]))


def rest_kernel(ordered, w_out, up_near, down_near, up_2, down_2, own, keep):
    side = up_2.shape[1]
    cut = 2 * side
    width = w_out.shape[1]
    small = keep.shape[0] // 4
    wide = 2 * small
    rows = jnp.concatenate(
        [
            ordered[(4 * half + step) * small : (4 * half + step + 1) * small, :]
            for step in (1, 3, 0)
            for half in range(2)
        ],
        axis=0,
    )
    for base, near, far in ((0, (down_near, 1), (up_2, 0)), (side, (up_near, 0), (down_2, 1))):
        for start, stop in pieces(base, base + side):
            result = dot(rows, w_out[:, start:stop]).astype(BF16)
            cols = slice(start - base, stop - base)
            for ref, at in (near, far):
                ref[:, cols] = result[at * wide : (at + 1) * wide]
            own[:, start:stop] = result[2 * wide :]
    for start, stop in pieces(cut, width):
        keep[:, start - cut : stop - cut] = dot(
            ordered[0 : 4 * small, :], w_out[:, start:stop]
        ).astype(BF16)


def add(left, right):
    return (left.astype(F32) + right.astype(F32)).astype(BF16)


def pass_on_kernel(up_2, down_2, up_1, down_1, up, down):
    up[...] = add(up_2[...], up_1[...])
    down[...] = add(down_2[...], down_1[...])


def swap_kernel(keep, swapped, after, block_0, block_1, block_2, block_3):
    size = block_0.shape[0]
    for step, block in enumerate((block_0, block_1, block_2, block_3)):
        rows = slice(step * size, (step + 1) * size)
        block[...] = add(keep[rows, :], swapped[rows, :])


def fold_kernel(own, up_near, down_near, up_2, down_2, after, kept, sent):
    small = kept.shape[0]
    total = ring_sum(own, up_near, down_near, up_2, down_2)
    kept[...] = total[:small]
    sent[...] = total[small:].astype(BF16)


def fetch_kernel(adapter, after, weights, sem):
    copy = pltpu.make_async_copy(adapter, weights, sem)
    copy.start()
    copy.wait()


def ring_sum(own, up_near, down_near, up_2, down_2):
    width = own.shape[1]
    side = width // 2
    left = own[:, 0:side].astype(F32) + down_near[...].astype(F32) + up_2[...].astype(F32)
    right = own[:, side:].astype(F32) + up_near[...].astype(F32) + down_2[...].astype(F32)
    return jnp.concatenate([left, right], axis=1)


def pool_kernel(
    rows, adapter, member, gain, features, kept, a_z, b_own, b_1, b_2, b_3, message, doc,
):
    small, width = rows.shape
    left = kept[...] + a_z[...].astype(F32)
    right = b_own[...].astype(F32) + b_1[...].astype(F32)
    right = right + b_2[...].astype(F32) + b_3[...].astype(F32)
    residual = jnp.concatenate([left, right], axis=1) + rows[...].astype(F32)
    norm = lax.rsqrt(jnp.sum(residual * residual, axis=1, keepdims=True) * (1.0 / width) + EPS)
    final = residual * norm * gain[...]
    means = dot(member[...], final, HIGH)
    doc[...] = means.astype(BF16)
    emb = adapter.shape[1]
    projected = dot(doc[...], adapter[...])
    projected = projected.astype(BF16)
    own = 32
    seqs = 16
    lane = lax.broadcasted_iota(jnp.int32, (DOCS_DEV, HD), 1) // own
    for peer in range(8):
        message[peer, :, 0:emb] = projected
        for group in range(seqs // 4):
            tile = None
            for slot in range(4):
                at = (2 * (group * 4 + slot) + peer // 4) * HD
                piece = means[:, at : at + HD]
                shift = ((slot - peer % 4) * own) % HD
                if shift:
                    piece = pltpu.roll(piece, shift, 1)
                tile = piece if tile is None else jnp.where(lane == slot, piece, tile)
            message[peer, :, emb + group * HD : emb + (group + 1) * HD] = tile.astype(BF16)
    image_rows = features[...].astype(F32)
    per_row = emb // HD
    lined = jnp.concatenate(
        [
            image_rows[row : row + 1, at * HD : (at + 1) * HD]
            for row in range(features.shape[0])
            for at in range(per_row)
        ],
        axis=0,
    ).astype(BF16)
    for peer in range(8):
        message[peer, :, emb + seqs * own :] = lined


def sum_kernel(message, second, images):
    emb = images.shape[1]
    cut = message.shape[2] - HD
    total = message[0, :, 0:cut].astype(F32)
    for peer in range(1, message.shape[0]):
        total = total + message[peer, :, 0:cut].astype(F32)
    total = total.astype(BF16)
    per_row = emb // HD
    for peer in range(message.shape[0]):
        lined = message[peer, :, cut:].astype(F32)
        for at in range(lined.shape[0]):
            row = peer * (lined.shape[0] // per_row) + at // per_row
            lane = (at % per_row) * HD
            images[row : row + 1, lane : lane + HD] = lined[at : at + 1, :]
    image_rows = images[...].astype(BF16)
    for chip in range(second.shape[0]):
        second[chip, :, 0:emb] = total[:, 0:emb]
        at = emb + (chip // 2) * HD
        second[chip, :, emb : emb + HD] = total[:, at : at + HD]
        second[chip, :, emb + HD :] = image_rows


def image_tower(values, gain, shift):
    center = values - jnp.mean(values, axis=1, keepdims=True)
    spread = lax.rsqrt(jnp.mean(center * center, axis=1, keepdims=True) + EPS)
    unit = center * spread
    normal = unit * gain + shift
    scale = lax.rsqrt(jnp.sum(normal * normal, axis=1, keepdims=True) + 1e-06)
    return unit, spread, normal * scale, scale


def split(value):
    high = value.astype(BF16)
    return high, (value - high.astype(F32)).astype(BF16)


def loss_kernel(
    same, other, features, ln_gain, ln_bias, pairs, loss, adapter_grad, feature_grad, all_rows, wide
):
    count = all_rows.shape[0]
    emb = features.shape[1]
    core = lax.rem(lax.axis_index("dp"), 2)
    for chip in range(count // (2 * DOCS_DEV)):
        rows = slice(chip * DOCS_DEV, (chip + 1) * DOCS_DEV)
        for ref, at in ((same, core), (other, 1 - core)):
            start = pl.multiple_of((2 * chip + at) * DOCS_DEV, DOCS_DEV)
            all_rows[pl.ds(start, DOCS_DEV), :] = ref[rows, :]
    image = image_tower(all_rows[:, emb + HD :].astype(F32), ln_gain[...], ln_bias[...])[2]
    image_high, image_low = split(image)
    narrow = all_rows[:, 0:emb]
    projected = narrow.astype(F32)
    text_scale = lax.rsqrt(jnp.sum(projected * projected, axis=1, keepdims=True) + 1e-06)
    text = projected * text_scale
    scores = (SCALE * text_scale) * (dot_rows(narrow, image_high) + dot_rows(narrow, image_low))
    grown = jnp.exp(scores)
    text_sum = jnp.sum(grown, axis=1, keepdims=True)
    image_sum = jnp.sum(grown, axis=0, keepdims=True)
    match = (lax.broadcasted_iota(jnp.int32, (count, count), 0) == pairs[...]).astype(F32)
    loss[...] = (
        jnp.sum(jnp.log(text_sum), axis=0, keepdims=True)
        + jnp.sum(jnp.log(image_sum), axis=1, keepdims=True)
        - 2.0 * jnp.sum(jnp.sum(scores * match, axis=1, keepdims=True), axis=0, keepdims=True)
    ) * (1.0 / (2.0 * count))
    dual = 0.5 * grown * (1.0 / text_sum + 1.0 / image_sum) - match
    dual_high, dual_low = split(dual)
    grad_text = SCALE * (
        dot(dual_high, image_high) + dot(dual_high, image_low) + dot(dual_low, image_high)
    )
    grad_projected = text_scale * (
        grad_text - text * jnp.sum(grad_text * text, axis=1, keepdims=True)
    )
    grad_high, grad_low = split(grad_projected)
    pooled = all_rows[:, emb : emb + HD].astype(F32).T.astype(BF16)
    wide[...] = dot(pooled, grad_high) + dot(pooled, grad_low)
    own = adapter_grad.shape[0]
    slot = pl.multiple_of(lax.rem(lax.axis_index("dp"), 4) * own, own)
    adapter_grad[...] = wide[pl.ds(slot, own), :]
    few = features.shape[0]
    chosen = (
        lax.broadcasted_iota(jnp.int32, (few, count), 1)
        == lax.axis_index(("dp", "mp")) * few + lax.broadcasted_iota(jnp.int32, (few, count), 0)
    ).astype(BF16)
    dual_own = dot_rows(chosen, dual_high) + dot_rows(chosen, dual_low)
    own_high, own_low = split(dual_own)
    text_high, text_low = split(text)
    grad_image = SCALE * (
        dot(own_high, text_high) + dot(own_high, text_low) + dot(own_low, text_high)
    )
    unit, spread, mine, scale = image_tower(
        features[...].astype(F32), ln_gain[...], ln_bias[...]
    )
    grad_normal = scale * (grad_image - mine * jnp.sum(grad_image * mine, axis=1, keepdims=True))
    grad_unit = grad_normal * ln_gain[...]
    feature_grad[...] = spread * (
        grad_unit
        - jnp.mean(grad_unit, axis=1, keepdims=True)
        - unit * jnp.mean(grad_unit * unit, axis=1, keepdims=True)
    )


def y_shift(step):
    return [(y * 2 + z, ((y + step) % 4) * 2 + z) for y in range(4) for z in range(2)]


Z_SWAP = [(m, m ^ 1) for m in range(8)]


def on_device(
    hidden,
    segment_ids,
    attn_gain,
    w_query,
    w_key,
    w_value,
    w_out,
    final_gain,
    adapter,
    features,
    ln_gain,
    ln_bias,
    pair_ids,
):
    length, width = hidden.shape
    emb_rows, emb = features.shape
    tensor_count = lax.axis_size("mp")
    seqs = lax.axis_size("dp")
    mine = lax.axis_index("mp")
    params = pltpu.CompilerParams(vmem_limit_bytes=16 * 1024 * 1024)
    roomy = pltpu.CompilerParams(vmem_limit_bytes=56 * 1024 * 1024)
    whole = pl.BlockSpec(memory_space=pltpu.VMEM)
    anywhere = pl.BlockSpec(memory_space=pl.ANY)
    far = pl.BlockSpec(memory_space=pltpu.HBM)
    small = length // 8
    cut = 2304
    q_cols = w_query.shape[1]
    kv_cols = w_key.shape[1]
    cosine, sine = rope_tables(length)
    late = jax.ShapeDtypeStruct((4 * small, width - cut), BF16)
    one = jax.ShapeDtypeStruct((2 * small, cut // 2), BF16)
    early = jax.ShapeDtypeStruct((2 * small, cut), BF16)
    send, up_1, down_1, ordered = pl.pallas_call(
        text_kernel,
        out_shape=[late, one, one, jax.ShapeDtypeStruct((length, q_cols), BF16)],
        in_specs=[far] * 5 + [whole, far, far, whole],
        out_specs=[anywhere] * 4,
        scratch_shapes=[
            pltpu.VMEM((length, width), BF16),
            pltpu.VMEM((width, q_cols + 2 * kv_cols), BF16),
            pltpu.VMEM((q_cols, width), BF16),
            pltpu.VMEM((2, length, HD), F32),
            pltpu.VMEM((length, q_cols + 2 * kv_cols), F32),
            pltpu.VMEM((length, q_cols), BF16),
            pltpu.VMEM((length, kv_cols), BF16),
            pltpu.VMEM((length, 2 * kv_cols), BF16),
            pltpu.VMEM((length, q_cols), BF16),
            pltpu.VMEM((length, q_cols), BF16),
            pltpu.VMEM((2 * small, cut), BF16),
            pltpu.VMEM(late.shape, BF16),
            pltpu.SemaphoreType.DMA((5, 4)),
            pltpu.SemaphoreType.DMA((4,)),
        ],
        compiler_params=pltpu.CompilerParams(vmem_limit_bytes=56 * 1024 * 1024),
        name="text_tower",
    )(
        hidden, w_query, w_key, w_value, w_out, attn_gain.reshape(1, width),
        jnp.asarray(cosine), jnp.asarray(sine), segment_ids,
    )
    swapped = lax.ppermute(send, "mp", Z_SWAP)
    up_1 = lax.ppermute(up_1, "mp", y_shift(1))
    down_1 = lax.ppermute(down_1, "mp", y_shift(3))
    up_near, down_near, up_2, down_2, a_own, keep = pl.pallas_call(
        rest_kernel,
        out_shape=[one] * 4 + [early, late],
        in_specs=[whole] * 2,
        out_specs=[whole] * 6,
        compiler_params=pltpu.CompilerParams(vmem_limit_bytes=24 * 1024 * 1024),
        cost_estimate=pl.CostEstimate(
            flops=length * q_cols * width, bytes_accessed=4 * q_cols * width, transcendentals=0
        ),
        name="other_terms",
    )(ordered, w_out)
    up_near = lax.ppermute(up_near, "mp", y_shift(1))
    down_near = lax.ppermute(down_near, "mp", y_shift(3))
    rows = lax.dynamic_slice_in_dim(hidden, mine * small, small, 0)
    up_2, rows = lax.optimization_barrier((up_2, rows))
    up_2, down_2 = pl.pallas_call(
        pass_on_kernel,
        out_shape=[one, one],
        in_specs=[whole] * 4,
        out_specs=[whole] * 2,
        compiler_params=params,
        name="pass_on",
    )(up_2, down_2, up_1, down_1)
    r_up = lax.ppermute(up_2, "mp", y_shift(1))
    r_down = lax.ppermute(down_2, "mp", y_shift(3))
    weights = pl.pallas_call(
        fetch_kernel,
        out_shape=jax.ShapeDtypeStruct(adapter.shape, BF16),
        in_specs=[anywhere] * 2,
        out_specs=whole,
        scratch_shapes=[pltpu.SemaphoreType.DMA],
        compiler_params=params,
        name="fetch_weights",
    )(adapter, up_2)
    blocks = pl.pallas_call(
        swap_kernel,
        out_shape=[jax.ShapeDtypeStruct((small, width - cut), BF16)] * 4,
        in_specs=[whole] * 2 + [anywhere],
        out_specs=[whole] * 4,
        compiler_params=params,
        name="add_swapped",
    )(keep, swapped, weights)
    q_2 = lax.ppermute(blocks[2], "mp", y_shift(2))
    q_1 = lax.ppermute(blocks[1], "mp", y_shift(1))
    q_3 = lax.ppermute(blocks[3], "mp", y_shift(3))
    kept, sent = pl.pallas_call(
        fold_kernel,
        out_shape=[
            jax.ShapeDtypeStruct((small, cut), F32),
            jax.ShapeDtypeStruct((small, cut), BF16),
        ],
        in_specs=[whole] * 5 + [anywhere],
        out_specs=[whole] * 2,
        compiler_params=params,
        name="fold",
    )(a_own, up_near, down_near, r_up, r_down, blocks[2])
    a_z = lax.ppermute(sent, "mp", Z_SWAP)
    seg = segment_ids[0]
    docs = jnp.arange(DOCS_DEV, dtype=jnp.int32)[:, None]
    counts = jnp.sum((docs == seg[None, :]).astype(F32), axis=1, keepdims=True)
    seg_rows = lax.dynamic_slice_in_dim(seg, mine * small, small, 0)
    member = (docs == seg_rows[None, :]).astype(F32) / counts
    own_cols = width // tensor_count
    chips = seqs // 2
    message = pl.pallas_call(
        pool_kernel,
        out_shape=jax.ShapeDtypeStruct((tensor_count, DOCS_DEV, emb + own_cols + HD), BF16),
        in_specs=[whole] * 11,
        out_specs=whole,
        scratch_shapes=[pltpu.VMEM((DOCS_DEV, width), BF16)],
        compiler_params=params,
        name="pool_and_project",
    )(
        rows, weights, member, final_gain.reshape(1, width), features,
        kept, a_z, blocks[0], q_1, q_2, q_3,
    )
    message = lax.all_to_all(message, "mp", 0, 0, tiled=True)
    second = pl.pallas_call(
        sum_kernel,
        out_shape=jax.ShapeDtypeStruct((chips, DOCS_DEV, 2 * emb + HD), BF16),
        in_specs=[whole],
        out_specs=whole,
        scratch_shapes=[pltpu.VMEM((DOCS_DEV, emb), F32)],
        compiler_params=params,
        name="sum_partials",
    )(message)
    second = lax.all_to_all(
        second, "dp", 0, 0, tiled=True,
        axis_index_groups=[[2 * chip + core for chip in range(chips)] for core in range(2)],
    ).reshape(chips * DOCS_DEV, 2 * emb + HD)
    other = lax.ppermute(second, "dp", [(d, d ^ 1) for d in range(seqs)])
    count = seqs * DOCS_DEV
    own = width // (seqs * tensor_count)
    loss, adapter_grad, feature_grad = pl.pallas_call(
        loss_kernel,
        out_shape=[
            jax.ShapeDtypeStruct((1, 1), F32),
            jax.ShapeDtypeStruct((own, emb), F32),
            jax.ShapeDtypeStruct((emb_rows, emb), F32),
        ],
        in_specs=[whole] * 6,
        out_specs=[whole] * 3,
        scratch_shapes=[pltpu.VMEM((count, 2 * emb + HD), BF16), pltpu.VMEM((HD, emb), F32)],
        compiler_params=params,
        name="loss_and_gradients",
    )(
        second, other, features,
        ln_gain.reshape(1, emb), ln_bias.reshape(1, emb), pair_ids.reshape(1, count),
    )
    return (loss[0, 0], adapter_grad, feature_grad)


def solution(mesh):
    return jax.shard_map(
        on_device,
        mesh=mesh,
        in_specs=(
            P("dp", None),
            P("dp", None),
            P(),
            P(None, "mp"),
            P(None, "mp"),
            P(None, "mp"),
            P("mp", None),
            P(),
            P(),
            P(("dp", "mp"), None),
            P(),
            P(),
            P(),
        ),
        out_specs=(P(), P(("dp", "mp"), None), P(("dp", "mp"), None)),
        check_vma=False,
    )
```

profile of v0, /device:TPU:1, one launch (start us, length us, event | category | flops | bytes accessed | tf_op | source)
XLA Modules:
  0.0 89.3 jit_solution(8760411598585330207)
XLA Ops:
  0.6 0.0 copy-start
  0.6 11.8 %text_tower.1 = (bf16[256,1792]{1,0:T(8,128)(2,1)}, bf16[128,1152]{1,0:T(8,128)(2,1)}, bf16[128,1152]{1,0:T(8,128)(2,1)}, bf16[512,512]{1,0:T(8,128)(2,1)}) custom-call(bf16[512,4096]{1,0:T(8,128)(2,1)} %hidden.1, bf16[4096,512]{1,0:T(8,128)(2,1)} %w_query.1, bf16[4096,128]{1,0:T(8,128)(2,1)} %w_key.1, bf16[4096,128]{1,0:T(8,128)(2,1)} %w_value.1, ...), custom_call_target="tpu_custom_call" | custom-call | tf_op jit(solution)/shard_map/text_tower/pallas_call | solution.py:422
  12.4 0.0 copy-start.12
  12.4 4.5 %collective-permute-start.6 = (bf16[256,1792]{1,0:T(8,128)(2,1)}, bf16[256,1792]{1,0:T(8,128)(2,1)S(1)}, u32[]{:S(2)}, u32[]{:S(2)}) collective-permute-start(bf16[256,1792]{1,0:T(8,128)(2,1)} %get-tuple-element.39), channel_id=1, source_target_pairs={{0,1},{1,0},{2,3},{3,2},{4,5},{5,4},{6,7},{7,6},{8,9},{9,8},{10,11... | collective-permute-start | bytes 2752520 | tf_op jit(solution)/shard_map/ppermute | solution.py:449
  17.0 1.3 %collective-permute-start = (bf16[128,1152]{1,0:T(8,128)(2,1)}, bf16[128,1152]{1,0:T(8,128)(2,1)S(1)}, u32[]{:S(2)}, u32[]{:S(2)}) collective-permute-start(bf16[128,1152]{1,0:T(8,128)(2,1)} %get-tuple-element.31), channel_id=1, source_target_pairs={{0,2},{1,3},{2,4},{3,5},{4,6},{5,7},{6,0},{7,1},{8,10},{9,11},{10,... | collective-permute-start | bytes 884744 | tf_op jit(solution)/shard_map/ppermute | solution.py:450
  18.3 1.4 %collective-permute-start.1 = (bf16[128,1152]{1,0:T(8,128)(2,1)}, bf16[128,1152]{1,0:T(8,128)(2,1)}, u32[]{:S(2)}, u32[]{:S(2)}) collective-permute-start(bf16[128,1152]{1,0:T(8,128)(2,1)} %get-tuple-element.32), channel_id=1, source_target_pairs={{0,6},{1,7},{2,0},{3,1},{4,2},{5,3},{6,4},{7,5},{8,14},{9,15},{10,... | collective-permute-start | bytes 884744 | tf_op jit(solution)/shard_map/ppermute | solution.py:451
  19.7 0.0 copy-done
  19.7 0.0 copy-start.2
  19.7 1.0 %copy-done.2 = bf16[512,512]{1,0:T(8,128)(2,1)S(1)} copy-done((bf16[512,512]{1,0:T(8,128)(2,1)S(1)}, bf16[512,512]{1,0:T(8,128)(2,1)}, u32[]{:S(2)}) %copy-start.2) | copy-done | bytes 524312
  20.7 1.9 %other_terms.1 = (bf16[128,1152]{1,0:T(8,128)(2,1)}, bf16[128,1152]{1,0:T(8,128)(2,1)}, bf16[128,1152]{1,0:T(8,128)(2,1)S(1)}, bf16[128,1152]{1,0:T(8,128)(2,1)S...) custom-call(bf16[512,512]{1,0:T(8,128)(2,1)S(1)} %copy-done.2, bf16[512,4096]{1,0:T(8,128)(2,1)S(1)} %copy-done), custom_call_target="tpu_custom_call" | custom-call | flops 1073741824 | bytes 8388608 | tf_op jit(solution)/shard_map/other_terms/pallas_call | solution.py:452
  22.7 0.0 copy-start.3
  22.7 0.7 copy-done.3
  23.4 0.0 copy-start.5
  23.4 0.7 copy-done.5
  24.1 0.0 collective-permute-start.2
  24.1 2.7 %collective-permute-start.3 = (bf16[128,1152]{1,0:T(8,128)(2,1)}, bf16[128,1152]{1,0:T(8,128)(2,1)S(1)}, u32[]{:S(2)}, u32[]{:S(2)}) collective-permute-start(bf16[128,1152]{1,0:T(8,128)(2,1)} %get-tuple-element.36), channel_id=1, source_target_pairs={{0,6},{1,7},{2,0},{3,1},{4,2},{5,3},{6,4},{7,5},{8,14},{9,15},{10,... | collective-permute-start | bytes 884744 | tf_op jit(solution)/shard_map/ppermute | solution.py:464
  26.8 1.1 %constant_dynamic-slice_fusion.rows = bf16[64,4096]{1,0:T(8,128)(2,1)S(1)} fusion(bf16[512,4096]{1,0:T(8,128)(2,1)} %hidden.1, s32[]{:T(128)S(6)} %select_n.4), kind=kLoop, calls=%fused_computation.5 | loop fusion | bytes 1048580 | tf_op jit(solution)/shard_map/dynamic_slice | solution.py:465
  27.9 0.0 collective-permute-done.up_1
  27.9 0.0 collective-permute-done.1.down_1
  27.9 0.0 copy-start.4
  27.9 1.0 %copy-done.4 = bf16[128,1152]{1,0:T(8,128)(2,1)S(1)} copy-done((bf16[128,1152]{1,0:T(8,128)(2,1)S(1)}, bf16[128,1152]{1,0:T(8,128)(2,1)}, u32[]{:S(2)}) %copy-start.4) | copy-done | bytes 294936
  28.9 0.0 copy-start.6
  28.9 1.0 %copy-done.6 = bf16[128,1152]{1,0:T(8,128)(2,1)S(1)} copy-done((bf16[128,1152]{1,0:T(8,128)(2,1)S(1)}, bf16[128,1152]{1,0:T(8,128)(2,1)}, u32[]{:S(2)}) %copy-start.6) | copy-done | bytes 294936
  29.8 1.1 %pass_on.1 = (bf16[128,1152]{1,0:T(8,128)(2,1)S(1)}, bf16[128,1152]{1,0:T(8,128)(2,1)S(1)}) custom-call(bf16[128,1152]{1,0:T(8,128)(2,1)S(1)} %copy-done.4, bf16[128,1152]{1,0:T(8,128)(2,1)S(1)} %copy-done.6, bf16[128,1152]{1,0:T(8,128)(2,1)S(1)} %collective-permute-done.up_1, bf16[128,1152]{1,0:T(8,128)(2,1)} %collective-permute-done.1.down_1), custom_call_target="tpu_custom_call" | custom-call | tf_op jit(solution)/shard_map/pass_on/pallas_call | solution.py:467
  30.9 0.7 collective-permute-start.5
  31.6 0.8 collective-permute-start.4
  32.5 0.0 copy-done.12
  32.5 0.1 convert_reduce_fusion
  32.6 0.0 copy-start.1
  32.6 3.4 %copy-done.1 = bf16[4096,1024]{1,0:T(8,128)(2,1)S(1)} copy-done((bf16[4096,1024]{1,0:T(8,128)(2,1)S(1)}, bf16[4096,1024]{1,0:T(8,128)(2,1)}, u32[]{:S(2)}) %copy-start.1) | copy-done | bytes 8388632
  36.0 0.6 fetch_weights.1.after.adapter
  36.5 0.7 collective-permute-done.6.swapped
  37.2 0.0 copy-start.8
  37.2 0.2 add_swapped.1
  37.5 1.4 %collective-permute-start.8 = (bf16[64,1792]{1,0:T(8,128)(2,1)S(1)}, bf16[64,1792]{1,0:T(8,128)(2,1)S(1)}, u32[]{:S(2)}, u32[]{:S(2)}) collective-permute-start(bf16[64,1792]{1,0:T(8,128)(2,1)S(1)} %get-tuple-element.44), channel_id=1, source_target_pairs={{0,2},{1,3},{2,4},{3,5},{4,6},{5,7},{6,0},{7,1},{8,10},{9,11},{10,... | collective-permute-start | bytes 688136 | tf_op jit(solution)/shard_map/ppermute | solution.py:495
  38.8 0.0 collective-permute-done.2.up_near
  38.8 1.7 %collective-permute-start.10 = (bf16[64,1792]{1,0:T(8,128)(2,1)S(1)}, bf16[64,1792]{1,0:T(8,128)(2,1)S(1)}, u32[]{:S(2)}, u32[]{:S(2)}) collective-permute-start(bf16[64,1792]{1,0:T(8,128)(2,1)S(1)} %get-tuple-element.45), channel_id=1, source_target_pairs={{0,6},{1,7},{2,0},{3,1},{4,2},{5,3},{6,4},{7,5},{8,14},{9,15},{10,... | collective-permute-start | bytes 688136 | tf_op jit(solution)/shard_map/ppermute | solution.py:496
  40.5 0.0 collective-permute-done.3.down_near
  40.5 1.4 %collective-permute-start.9 = (bf16[64,1792]{1,0:T(8,128)(2,1)S(1)}, bf16[64,1792]{1,0:T(8,128)(2,1)S(1)}, u32[]{:S(2)}, u32[]{:S(2)}) collective-permute-start(bf16[64,1792]{1,0:T(8,128)(2,1)S(1)} %get-tuple-element.40.after), channel_id=1, source_target_pairs={{0,4},{1,5},{2,6},{3,7},{4,0},{5,1},{6,2},{7,3},{8,12},{9,13},{10,... | collective-permute-start | bytes 688136 | tf_op jit(solution)/shard_map/ppermute | solution.py:494
  41.9 0.0 collective-permute-done.5.down_2
  41.9 0.0 collective-permute-done.4.up_2
  41.9 0.2 fold.1
  42.1 2.7 %collective-permute-start.7 = (bf16[64,2304]{1,0:T(8,128)(2,1)S(1)}, bf16[64,2304]{1,0:T(8,128)(2,1)S(1)}, u32[]{:S(2)}, u32[]{:S(2)}) collective-permute-start(bf16[64,2304]{1,0:T(8,128)(2,1)S(1)} %get-tuple-element.42), channel_id=1, source_target_pairs={{0,1},{1,0},{2,3},{3,2},{4,5},{5,4},{6,7},{7,6},{8,9},{9,8},{10,11... | collective-permute-start | bytes 884744 | tf_op jit(solution)/shard_map/ppermute | solution.py:508
  44.9 0.1 dynamic-slice_bitcast_fusion
  44.9 0.1 convert_divide_fusion.member
  45.0 0.0 collective-permute-done.8.b_1
  45.0 0.0 collective-permute-done.10.b_3
  45.0 5.7 %collective-permute-done.9.b_2 = bf16[64,1792]{1,0:T(8,128)(2,1)S(1)} collective-permute-done((bf16[64,1792]{1,0:T(8,128)(2,1)S(1)}, bf16[64,1792]{1,0:T(8,128)(2,1)S(1)}, u32[]{:S(2)}, u32[]{:S(2)}) %collective-permute-start.9) | collective-permute-done | bytes 229408 | tf_op jit(solution)/shard_map/ppermute | solution.py:494
  50.8 0.0 collective-permute-done.7.a_z
  50.8 0.0 copy-done.7
  50.8 0.0 copy-done.8
  50.8 0.0 copy-start.9
  50.8 0.0 copy-start.10
  50.8 0.0 copy-start.11
  50.8 2.0 %pool_and_project.1 = bf16[8,16,1664]{2,1,0:T(8,128)(2,1)S(1)} custom-call(bf16[64,4096]{1,0:T(8,128)(2,1)S(1)} %constant_dynamic-slice_fusion.rows, bf16[4096,1024]{1,0:T(8,128)(2,1)S(1)} %fetch_weights.1.after.adapter, f32[16,64]{1,0:T(8,128)S(1)} %convert_divide_fusion.member, f32[1,4096]{1,0:T(1,128)S(1)} %bitcast.12, bf16[2,1024]{1,0:T(2,128)(2,1)S(1)} %copy-done.8, ...), custom_call_target="tpu_custom_call" | custom-call | tf_op jit(solution)/shard_map/pool_and_project/pallas_call | solution.py:516
  52.8 12.8 %all_to_all.10.message = bf16[8,16,1664]{2,1,0:T(8,128)(2,1)S(1)} all-to-all(bf16[8,16,1664]{2,1,0:T(8,128)(2,1)S(1)} %pool_and_project.1), channel_id=1, replica_groups=mesh['dp'=16,'mp'=8] {'mp'}, dimensions={0} | all-to-all | bytes 851968 | tf_op jit(solution)/shard_map/all_to_all | solution.py:528
  65.6 0.1 sum_partials.1
  65.7 12.3 %all_to_all.11 = bf16[8,16,2176]{2,1,0:T(8,128)(2,1)S(1)} all-to-all(bf16[8,16,2176]{2,1,0:T(8,128)(2,1)S(1)} %sum_partials.1), channel_id=1, replica_groups={{0,16,32,48,64,80,96,112},{8,24,40,56,72,88,104,120},{1,17,33,49,65,81,..., dimensions={0} | all-to-all | bytes 1114112 | tf_op jit(solution)/shard_map/all_to_all | solution.py:538
  78.0 5.7 %collective-permute-start.11 = (bf16[128,2176]{1,0:T(8,128)(2,1)S(1)}, bf16[128,2176]{1,0:T(8,128)(2,1)S(1)}, u32[]{:S(2)}, u32[]{:S(2)}) collective-permute-start(bf16[128,2176]{1,0:T(8,128)(2,1)S(1)} %bitcast.10), channel_id=1, source_target_pairs={{0,8},{8,0},{16,24},{24,16},{32,40},{40,32},{48,56},{56,48},{64,72... | collective-permute-start | bytes 1671176 | tf_op jit(solution)/shard_map/ppermute | solution.py:542
  83.7 1.6 %collective-permute-done.11.other = bf16[128,2176]{1,0:T(8,128)(2,1)S(1)} collective-permute-done((bf16[128,2176]{1,0:T(8,128)(2,1)S(1)}, bf16[128,2176]{1,0:T(8,128)(2,1)S(1)}, u32[]{:S(2)}, u32[]{:S(2)}) %collective-permute-start.11) | collective-permute-done | bytes 557088 | tf_op jit(solution)/shard_map/ppermute | solution.py:542
  85.3 0.0 copy-done.9
  85.3 0.0 copy-done.10
  85.3 0.0 copy-done.11
  85.3 3.9 %loss_and_gradients.1 = (f32[1,1]{1,0:T(1,128)}, f32[32,1024]{1,0:T(8,128)}, f32[2,1024]{1,0:T(2,128)}) custom-call(bf16[128,2176]{1,0:T(8,128)(2,1)S(1)} %bitcast.11, bf16[128,2176]{1,0:T(8,128)(2,1)S(1)} %collective-permute-done.11.other, bf16[2,1024]{1,0:T(2,128)(2,1)S(1)} %copy-done.8, f32[1,1024]{1,0:T(1,128)S(1)} %bitcast.13, f32[1,1024]{1,0:T(1,128)S(1)} %bitcast.14, ...), custom_call_target="tpu_custom_call" | custom-call | tf_op jit(solution)/shard_map/loss_and_gradients/pallas_call | solution.py:545
  (1 shorter events, 0.0 us)
Async XLA Ops:
  0.6 19.1 %copy-start = (bf16[512,4096]{1,0:T(8,128)(2,1)S(1)}, bf16[512,4096]{1,0:T(8,128)(2,1)}, u32[]{:S(2)}) copy-start(bf16[512,4096]{1,0:T(8,128)(2,1)} %w_out.3) | copy-start | bytes 12582916
  12.4 20.0 %copy-start.12 = (s32[1,512]{1,0:T(1,128)S(1)}, s32[1,512]{1,0:T(1,128)}, u32[]{:S(2)}) copy-start(s32[1,512]{1,0:T(1,128)} %seg.1) | copy-start | bytes 6148
  12.4 24.8 %collective-permute-start.6 = (bf16[256,1792]{1,0:T(8,128)(2,1)}, bf16[256,1792]{1,0:T(8,128)(2,1)S(1)}, u32[]{:S(2)}, u32[]{:S(2)}) collective-permute-start(bf16[256,1792]{1,0:T(8,128)(2,1)} %get-tuple-element.39), channel_id=1, source_target_pairs={{0,1},{1,0},{2,3},{3,2},{4,5},{5,4},{6,7},{7,6},{8,9},{9,8},{10,11... | collective-permute-start | bytes 2752520 | tf_op jit(solution)/shard_map/ppermute | solution.py:449
  17.0 10.9 %collective-permute-start = (bf16[128,1152]{1,0:T(8,128)(2,1)}, bf16[128,1152]{1,0:T(8,128)(2,1)S(1)}, u32[]{:S(2)}, u32[]{:S(2)}) collective-permute-start(bf16[128,1152]{1,0:T(8,128)(2,1)} %get-tuple-element.31), channel_id=1, source_target_pairs={{0,2},{1,3},{2,4},{3,5},{4,6},{5,7},{6,0},{7,1},{8,10},{9,11},{10,... | collective-permute-start | bytes 884744 | tf_op jit(solution)/shard_map/ppermute | solution.py:450
  18.3 9.6 %collective-permute-start.1 = (bf16[128,1152]{1,0:T(8,128)(2,1)}, bf16[128,1152]{1,0:T(8,128)(2,1)}, u32[]{:S(2)}, u32[]{:S(2)}) collective-permute-start(bf16[128,1152]{1,0:T(8,128)(2,1)} %get-tuple-element.32), channel_id=1, source_target_pairs={{0,6},{1,7},{2,0},{3,1},{4,2},{5,3},{6,4},{7,5},{8,14},{9,15},{10,... | collective-permute-start | bytes 884744 | tf_op jit(solution)/shard_map/ppermute | solution.py:451
  19.7 1.0 %copy-start.2 = (bf16[512,512]{1,0:T(8,128)(2,1)S(1)}, bf16[512,512]{1,0:T(8,128)(2,1)}, u32[]{:S(2)}) copy-start(bf16[512,512]{1,0:T(8,128)(2,1)} %get-tuple-element.26.ordered) | copy-start | bytes 1572868
  22.7 0.7 copy-start.3
  23.4 0.7 copy-start.5
  24.1 14.7 %collective-permute-start.2 = (bf16[128,1152]{1,0:T(8,128)(2,1)}, bf16[128,1152]{1,0:T(8,128)(2,1)S(1)}, u32[]{:S(2)}, u32[]{:S(2)}) collective-permute-start(bf16[128,1152]{1,0:T(8,128)(2,1)} %get-tuple-element.35), channel_id=1, source_target_pairs={{0,2},{1,3},{2,4},{3,5},{4,6},{5,7},{6,0},{7,1},{8,10},{9,11},{10,... | collective-permute-start | bytes 884744 | tf_op jit(solution)/shard_map/ppermute | solution.py:463
  24.1 16.4 %collective-permute-start.3 = (bf16[128,1152]{1,0:T(8,128)(2,1)}, bf16[128,1152]{1,0:T(8,128)(2,1)S(1)}, u32[]{:S(2)}, u32[]{:S(2)}) collective-permute-start(bf16[128,1152]{1,0:T(8,128)(2,1)} %get-tuple-element.36), channel_id=1, source_target_pairs={{0,6},{1,7},{2,0},{3,1},{4,2},{5,3},{6,4},{7,5},{8,14},{9,15},{10,... | collective-permute-start | bytes 884744 | tf_op jit(solution)/shard_map/ppermute | solution.py:464
  27.9 1.0 %copy-start.4 = (bf16[128,1152]{1,0:T(8,128)(2,1)S(1)}, bf16[128,1152]{1,0:T(8,128)(2,1)}, u32[]{:S(2)}) copy-start(bf16[128,1152]{1,0:T(8,128)(2,1)} %copy-done.3) | copy-start | bytes 884740
  28.9 1.0 %copy-start.6 = (bf16[128,1152]{1,0:T(8,128)(2,1)S(1)}, bf16[128,1152]{1,0:T(8,128)(2,1)}, u32[]{:S(2)}) copy-start(bf16[128,1152]{1,0:T(8,128)(2,1)} %copy-done.5) | copy-start | bytes 884740
  30.9 11.0 %collective-permute-start.5 = (bf16[128,1152]{1,0:T(8,128)(2,1)S(1)}, bf16[128,1152]{1,0:T(8,128)(2,1)S(1)}, u32[]{:S(2)}, u32[]{:S(2)}) collective-permute-start(bf16[128,1152]{1,0:T(8,128)(2,1)S(1)} %get-tuple-element.37), channel_id=1, source_target_pairs={{0,6},{1,7},{2,0},{3,1},{4,2},{5,3},{6,4},{7,5},{8,14},{9,15},{10,... | collective-permute-start | bytes 884744 | tf_op jit(solution)/shard_map/ppermute | solution.py:476
  31.6 10.3 %collective-permute-start.4 = (bf16[128,1152]{1,0:T(8,128)(2,1)S(1)}, bf16[128,1152]{1,0:T(8,128)(2,1)S(1)}, u32[]{:S(2)}, u32[]{:S(2)}) collective-permute-start(bf16[128,1152]{1,0:T(8,128)(2,1)S(1)} %get-tuple-element.33.after), channel_id=1, source_target_pairs={{0,2},{1,3},{2,4},{3,5},{4,6},{5,7},{6,0},{7,1},{8,10},{9,11},{10,... | collective-permute-start | bytes 884744 | tf_op jit(solution)/shard_map/ppermute | solution.py:475
  32.6 3.4 %copy-start.1 = (bf16[4096,1024]{1,0:T(8,128)(2,1)S(1)}, bf16[4096,1024]{1,0:T(8,128)(2,1)}, u32[]{:S(2)}) copy-start(bf16[4096,1024]{1,0:T(8,128)(2,1)} %adapter.1) | copy-start | bytes 25165828
  37.2 13.5 %copy-start.7 = (f32[4096]{0:T(1024)S(1)}, f32[4096]{0:T(1024)}, u32[]{:S(2)}) copy-start(f32[4096]{0:T(1024)} %param.22) | copy-start | bytes 49156
  37.2 13.5 %copy-start.8 = (bf16[2,1024]{1,0:T(2,128)(2,1)S(1)}, bf16[2,1024]{1,0:T(2,128)(2,1)}, u32[]{:S(2)}) copy-start(bf16[2,1024]{1,0:T(2,128)(2,1)} %features.3) | copy-start | bytes 12292
  37.5 7.6 %collective-permute-start.8 = (bf16[64,1792]{1,0:T(8,128)(2,1)S(1)}, bf16[64,1792]{1,0:T(8,128)(2,1)S(1)}, u32[]{:S(2)}, u32[]{:S(2)}) collective-permute-start(bf16[64,1792]{1,0:T(8,128)(2,1)S(1)} %get-tuple-element.44), channel_id=1, source_target_pairs={{0,2},{1,3},{2,4},{3,5},{4,6},{5,7},{6,0},{7,1},{8,10},{9,11},{10,... | collective-permute-start | bytes 688136 | tf_op jit(solution)/shard_map/ppermute | solution.py:495
  38.8 6.2 %collective-permute-start.10 = (bf16[64,1792]{1,0:T(8,128)(2,1)S(1)}, bf16[64,1792]{1,0:T(8,128)(2,1)S(1)}, u32[]{:S(2)}, u32[]{:S(2)}) collective-permute-start(bf16[64,1792]{1,0:T(8,128)(2,1)S(1)} %get-tuple-element.45), channel_id=1, source_target_pairs={{0,6},{1,7},{2,0},{3,1},{4,2},{5,3},{6,4},{7,5},{8,14},{9,15},{10,... | collective-permute-start | bytes 688136 | tf_op jit(solution)/shard_map/ppermute | solution.py:496
  40.5 10.2 %collective-permute-start.9 = (bf16[64,1792]{1,0:T(8,128)(2,1)S(1)}, bf16[64,1792]{1,0:T(8,128)(2,1)S(1)}, u32[]{:S(2)}, u32[]{:S(2)}) collective-permute-start(bf16[64,1792]{1,0:T(8,128)(2,1)S(1)} %get-tuple-element.40.after), channel_id=1, source_target_pairs={{0,4},{1,5},{2,6},{3,7},{4,0},{5,1},{6,2},{7,3},{8,12},{9,13},{10,... | collective-permute-start | bytes 688136 | tf_op jit(solution)/shard_map/ppermute | solution.py:494
  42.1 8.6 %collective-permute-start.7 = (bf16[64,2304]{1,0:T(8,128)(2,1)S(1)}, bf16[64,2304]{1,0:T(8,128)(2,1)S(1)}, u32[]{:S(2)}, u32[]{:S(2)}) collective-permute-start(bf16[64,2304]{1,0:T(8,128)(2,1)S(1)} %get-tuple-element.42), channel_id=1, source_target_pairs={{0,1},{1,0},{2,3},{3,2},{4,5},{5,4},{6,7},{7,6},{8,9},{9,8},{10,11... | collective-permute-start | bytes 884744 | tf_op jit(solution)/shard_map/ppermute | solution.py:508
  50.8 34.5 %copy-start.9 = (f32[1024]{0:T(1024)S(1)}, f32[1024]{0:T(1024)}, u32[]{:S(2)}) copy-start(f32[1024]{0:T(1024)} %param.25) | copy-start | bytes 12292
  50.8 34.5 %copy-start.10 = (f32[1024]{0:T(1024)S(1)}, f32[1024]{0:T(1024)}, u32[]{:S(2)}) copy-start(f32[1024]{0:T(1024)} %param.26) | copy-start | bytes 12292
  50.8 34.5 %copy-start.11 = (s32[256]{0:T(256)S(1)}, s32[256]{0:T(256)}, u32[]{:S(2)}) copy-start(s32[256]{0:T(256)} %param.27) | copy-start | bytes 3076
  78.0 7.3 %collective-permute-start.11 = (bf16[128,2176]{1,0:T(8,128)(2,1)S(1)}, bf16[128,2176]{1,0:T(8,128)(2,1)S(1)}, u32[]{:S(2)}, u32[]{:S(2)}) collective-permute-start(bf16[128,2176]{1,0:T(8,128)(2,1)S(1)} %bitcast.10), channel_id=1, source_target_pairs={{0,8},{8,0},{16,24},{24,16},{32,40},{40,32},{48,56},{56,48},{64,72... | collective-permute-start | bytes 1671176 | tf_op jit(solution)/shard_map/ppermute | solution.py:542
where the time goes:
time: 89.7 us; the launch traced here: 89.3 us
  blocking collectives  25.1 us (28%)
  starting transfers between devices  24.3 us (27%)
  Pallas kernels  21.9 us (24%)
  local copies, waits for them, and re-layouts  8.98 us (10%)
  waiting for transfers between devices  8.04 us (9%)
    all_to_all x1, blocking collectives, on_device(): message = lax.all_to_all(message, 'mp', 0, 0, tiled=True)  12.8 us
    all_to_all x1, blocking collectives, on_device(): lax.all_to_all(second, 'dp', 0, 0, tiled=True, axis_index_groups=[[2 * ch...  12.3 us
    pallas_call x1, Pallas kernels, on_device(): pl.pallas_call(text_kernel, out_shape=[late, one, one, jax.ShapeDtypeStru...  11.8 us
    unnamed x26, local copies, waits for them, and re-layouts  7.83 us
    ppermute x1, waiting for transfers between devices, on_device(): q_2 = lax.ppermute(blocks[2], 'mp', y_shift(2))  5.73 us
    ppermute x1, starting transfers between devices, on_device(): other = lax.ppermute(second, 'dp', [(d, d ^ 1) for d in range(seqs)])  5.69 us
    ppermute x1, starting transfers between devices, on_device(): swapped = lax.ppermute(send, 'mp', Z_SWAP)  4.5 us
    pallas_call x1, Pallas kernels, on_device(): pl.pallas_call(loss_kernel, out_shape=[jax.ShapeDtypeStruct((1, 1), F32),...  3.94 us
  transfers between devices with their start and end apart: 12, of which 3 were waited for; matrix products, arithmetic and copies ran while one was open for 2% of the time, Pallas kernels for 4%

commit v1 on v0

--- a/solution.py
+++ b/solution.py
@@ -171,7 +171,19 @@
     return list(zip(edges[:-1], edges[1:]))
 
 
-def rest_kernel(ordered, w_out, up_near, down_near, up_2, down_2, own, keep):
+def rest_kernel(
+    ordered, w_out, features, ln_gain, ln_bias, up_near, down_near, up_2, down_2, own, keep, lined
+):
+    image_rows = image_tower(features[...].astype(F32), ln_gain[...], ln_bias[...])[2]
+    per_row = features.shape[1] // HD
+    lined[...] = jnp.concatenate(
+        [
+            image_rows[row : row + 1, at * HD : (at + 1) * HD]
+            for row in range(features.shape[0])
+            for at in range(per_row)
+        ],
+        axis=0,
+    ).astype(BF16)
     side = up_2.shape[1]
     cut = 2 * side
     width = w_out.shape[1]
@@ -236,7 +248,7 @@
 
 
 def pool_kernel(
-    rows, adapter, member, gain, features, kept, a_z, b_own, b_1, b_2, b_3, message, doc,
+    rows, adapter, member, gain, lined, kept, a_z, b_own, b_1, b_2, b_3, message, doc,
 ):
     small, width = rows.shape
     left = kept[...] + a_z[...].astype(F32)
@@ -265,18 +277,8 @@
                     piece = pltpu.roll(piece, shift, 1)
                 tile = piece if tile is None else jnp.where(lane == slot, piece, tile)
             message[peer, :, emb + group * HD : emb + (group + 1) * HD] = tile.astype(BF16)
-    image_rows = features[...].astype(F32)
-    per_row = emb // HD
-    lined = jnp.concatenate(
-        [
-            image_rows[row : row + 1, at * HD : (at + 1) * HD]
-            for row in range(features.shape[0])
-            for at in range(per_row)
-        ],
-        axis=0,
-    ).astype(BF16)
     for peer in range(8):
-        message[peer, :, emb + seqs * own :] = lined
+        message[peer, :, emb + seqs * own :] = lined[...]
 
 
 def sum_kernel(message, second, images):
@@ -326,13 +328,12 @@
         for ref, at in ((same, core), (other, 1 - core)):
             start = pl.multiple_of((2 * chip + at) * DOCS_DEV, DOCS_DEV)
             all_rows[pl.ds(start, DOCS_DEV), :] = ref[rows, :]
-    image = image_tower(all_rows[:, emb + HD :].astype(F32), ln_gain[...], ln_bias[...])[2]
-    image_high, image_low = split(image)
+    image = all_rows[:, emb + HD :]
     narrow = all_rows[:, 0:emb]
     projected = narrow.astype(F32)
     text_scale = lax.rsqrt(jnp.sum(projected * projected, axis=1, keepdims=True) + 1e-06)
     text = projected * text_scale
-    scores = (SCALE * text_scale) * (dot_rows(narrow, image_high) + dot_rows(narrow, image_low))
+    scores = (SCALE * text_scale) * dot_rows(narrow, image)
     grown = jnp.exp(scores)
     text_sum = jnp.sum(grown, axis=1, keepdims=True)
     image_sum = jnp.sum(grown, axis=0, keepdims=True)
@@ -344,9 +345,7 @@
     ) * (1.0 / (2.0 * count))
     dual = 0.5 * grown * (1.0 / text_sum + 1.0 / image_sum) - match
     dual_high, dual_low = split(dual)
-    grad_text = SCALE * (
-        dot(dual_high, image_high) + dot(dual_high, image_low) + dot(dual_low, image_high)
-    )
+    grad_text = SCALE * (dot(dual_high, image) + dot(dual_low, image))
     grad_projected = text_scale * (
         grad_text - text * jnp.sum(grad_text * text, axis=1, keepdims=True)
     )
@@ -449,17 +448,17 @@
     swapped = lax.ppermute(send, "mp", Z_SWAP)
     up_1 = lax.ppermute(up_1, "mp", y_shift(1))
     down_1 = lax.ppermute(down_1, "mp", y_shift(3))
-    up_near, down_near, up_2, down_2, a_own, keep = pl.pallas_call(
+    up_near, down_near, up_2, down_2, a_own, keep, lined = pl.pallas_call(
         rest_kernel,
-        out_shape=[one] * 4 + [early, late],
-        in_specs=[whole] * 2,
-        out_specs=[whole] * 6,
+        out_shape=[one] * 4 + [early, late, jax.ShapeDtypeStruct((DOCS_DEV, HD), BF16)],
+        in_specs=[whole] * 5,
+        out_specs=[whole] * 7,
         compiler_params=pltpu.CompilerParams(vmem_limit_bytes=24 * 1024 * 1024),
         cost_estimate=pl.CostEstimate(
             flops=length * q_cols * width, bytes_accessed=4 * q_cols * width, transcendentals=0
         ),
         name="other_terms",
-    )(ordered, w_out)
+    )(ordered, w_out, features, ln_gain.reshape(1, emb), ln_bias.reshape(1, emb))
     up_near = lax.ppermute(up_near, "mp", y_shift(1))
     down_near = lax.ppermute(down_near, "mp", y_shift(3))
     rows = lax.dynamic_slice_in_dim(hidden, mine * small, small, 0)
@@ -522,7 +521,7 @@
         compiler_params=params,
         name="pool_and_project",
     )(
-        rows, weights, member, final_gain.reshape(1, width), features,
+        rows, weights, member, final_gain.reshape(1, width), lined,
         kept, a_z, blocks[0], q_1, q_2, q_3,
     )
     message = lax.all_to_all(message, "mp", 0, 0, tiled=True)

time: 89.7 us -> 88.9 us (level)
    pallas_call x1, Pallas kernels: 3.94 us -> 2.98 us  [on_device(): pl.pallas_call(loss_kernel, out_shape=[jax.ShapeDtypeStruct((1, 1), F32),...]
  transfers between devices with their start and end apart: 12 -> 12, of which waited for: 3 -> 3; matrix products, arithmetic and copies ran while one was open for 2% -> 2% of each run, Pallas kernels for 4% -> 5%
where the time goes in v1:
time: 88.9 us; the launch traced here: 88.5 us
  blocking collectives  25.1 us (28%)
  starting transfers between devices  24.3 us (27%)
  Pallas kernels  21.4 us (24%)
  local copies, waits for them, and re-layouts  8.96 us (10%)
  waiting for transfers between devices  7.8 us (9%)
    all_to_all x1, blocking collectives, on_device(): message = lax.all_to_all(message, 'mp', 0, 0, tiled=True)  12.8 us
    all_to_all x1, blocking collectives, on_device(): lax.all_to_all(second, 'dp', 0, 0, tiled=True, axis_index_groups=[[2 * ch...  12.3 us
    pallas_call x1, Pallas kernels, on_device(): pl.pallas_call(text_kernel, out_shape=[late, one, one, jax.ShapeDtypeStru...  12 us
    unnamed x26, local copies, waits for them, and re-layouts  7.82 us
    ppermute x1, waiting for transfers between devices, on_device(): q_2 = lax.ppermute(blocks[2], 'mp', y_shift(2))  5.74 us
    ppermute x1, starting transfers between devices, on_device(): other = lax.ppermute(second, 'dp', [(d, d ^ 1) for d in range(seqs)])  5.69 us
    ppermute x1, starting transfers between devices, on_device(): swapped = lax.ppermute(send, 'mp', Z_SWAP)  4.5 us
    pallas_call x1, Pallas kernels, on_device(): pl.pallas_call(loss_kernel, out_shape=[jax.ShapeDtypeStruct((1, 1), F32),...  2.98 us
  transfers between devices with their start and end apart: 12, of which 3 were waited for; matrix products, arithmetic and copies ran while one was open for 2% of the time, Pallas kernels for 5%

profile of v1, /device:TPU:1, one launch (start us, length us, event | category | flops | bytes accessed | tf_op | source)
XLA Modules:
  0.0 88.5 jit_solution(11736697030851391580)
XLA Ops:
  0.6 0.0 copy-start
  0.6 0.0 copy-start.8
  0.7 0.0 copy-start.9
  0.7 0.0 copy-start.10
  0.7 12.0 %text_tower.1 = (bf16[256,1792]{1,0:T(8,128)(2,1)}, bf16[128,1152]{1,0:T(8,128)(2,1)}, bf16[128,1152]{1,0:T(8,128)(2,1)}, bf16[512,512]{1,0:T(8,128)(2,1)}) custom-call(bf16[512,4096]{1,0:T(8,128)(2,1)} %hidden.1, bf16[4096,512]{1,0:T(8,128)(2,1)} %w_query.1, bf16[4096,128]{1,0:T(8,128)(2,1)} %w_key.1, bf16[4096,128]{1,0:T(8,128)(2,1)} %w_value.1, ...), custom_call_target="tpu_custom_call" | custom-call | tf_op jit(solution)/shard_map/text_tower/pallas_call | solution.py:421
  12.7 0.0 copy-start.12
  12.7 4.5 %collective-permute-start.6 = (bf16[256,1792]{1,0:T(8,128)(2,1)}, bf16[256,1792]{1,0:T(8,128)(2,1)S(1)}, u32[]{:S(2)}, u32[]{:S(2)}) collective-permute-start(bf16[256,1792]{1,0:T(8,128)(2,1)} %get-tuple-element.41), channel_id=1, source_target_pairs={{0,1},{1,0},{2,3},{3,2},{4,5},{5,4},{6,7},{7,6},{8,9},{9,8},{10,11... | collective-permute-start | bytes 2752520 | tf_op jit(solution)/shard_map/ppermute | solution.py:448
  17.2 1.3 %collective-permute-start = (bf16[128,1152]{1,0:T(8,128)(2,1)}, bf16[128,1152]{1,0:T(8,128)(2,1)S(1)}, u32[]{:S(2)}, u32[]{:S(2)}) collective-permute-start(bf16[128,1152]{1,0:T(8,128)(2,1)} %get-tuple-element.32), channel_id=1, source_target_pairs={{0,2},{1,3},{2,4},{3,5},{4,6},{5,7},{6,0},{7,1},{8,10},{9,11},{10,... | collective-permute-start | bytes 884744 | tf_op jit(solution)/shard_map/ppermute | solution.py:449
  18.5 1.4 %collective-permute-start.1 = (bf16[128,1152]{1,0:T(8,128)(2,1)}, bf16[128,1152]{1,0:T(8,128)(2,1)}, u32[]{:S(2)}, u32[]{:S(2)}) collective-permute-start(bf16[128,1152]{1,0:T(8,128)(2,1)} %get-tuple-element.33), channel_id=1, source_target_pairs={{0,6},{1,7},{2,0},{3,1},{4,2},{5,3},{6,4},{7,5},{8,14},{9,15},{10,... | collective-permute-start | bytes 884744 | tf_op jit(solution)/shard_map/ppermute | solution.py:450
  20.0 0.0 copy-done
  20.0 0.0 copy-done.8
  20.0 0.0 copy-done.9
  20.0 0.0 copy-done.10
  20.0 0.0 copy-start.2
  20.0 1.0 %copy-done.2 = bf16[512,512]{1,0:T(8,128)(2,1)S(1)} copy-done((bf16[512,512]{1,0:T(8,128)(2,1)S(1)}, bf16[512,512]{1,0:T(8,128)(2,1)}, u32[]{:S(2)}) %copy-start.2) | copy-done | bytes 524312
  21.0 2.1 %other_terms.1 = (bf16[128,1152]{1,0:T(8,128)(2,1)}, bf16[128,1152]{1,0:T(8,128)(2,1)}, bf16[128,1152]{1,0:T(8,128)(2,1)S(1)}, bf16[128,1152]{1,0:T(8,128)(2,1)S...) custom-call(bf16[512,512]{1,0:T(8,128)(2,1)S(1)} %copy-done.2, ...), custom_call_target="tpu_custom_call" | custom-call | flops 1073741824 | bytes 8388608 | tf_op jit(solution)/shard_map/other_terms/pallas_call | solution.py:451
  23.1 0.0 copy-start.3
  23.1 0.7 copy-done.3
  23.9 0.0 copy-start.5
  23.9 0.7 copy-done.5
  24.6 0.0 collective-permute-start.2
  24.6 2.7 %collective-permute-start.3 = (bf16[128,1152]{1,0:T(8,128)(2,1)}, bf16[128,1152]{1,0:T(8,128)(2,1)S(1)}, u32[]{:S(2)}, u32[]{:S(2)}) collective-permute-start(bf16[128,1152]{1,0:T(8,128)(2,1)} %get-tuple-element.38), channel_id=1, source_target_pairs={{0,6},{1,7},{2,0},{3,1},{4,2},{5,3},{6,4},{7,5},{8,14},{9,15},{10,... | collective-permute-start | bytes 884744 | tf_op jit(solution)/shard_map/ppermute | solution.py:463
  27.3 1.1 %constant_dynamic-slice_fusion.rows = bf16[64,4096]{1,0:T(8,128)(2,1)S(1)} fusion(bf16[512,4096]{1,0:T(8,128)(2,1)} %hidden.1, s32[]{:T(128)S(6)} %select_n.4), kind=kLoop, calls=%fused_computation.5 | loop fusion | bytes 1048580 | tf_op jit(solution)/shard_map/dynamic_slice | solution.py:464
  28.4 0.0 collective-permute-done.up_1
  28.4 0.0 collective-permute-done.1.down_1
  28.4 0.0 copy-start.4
  28.4 1.0 %copy-done.4 = bf16[128,1152]{1,0:T(8,128)(2,1)S(1)} copy-done((bf16[128,1152]{1,0:T(8,128)(2,1)S(1)}, bf16[128,1152]{1,0:T(8,128)(2,1)}, u32[]{:S(2)}) %copy-start.4) | copy-done | bytes 294936
  29.3 0.0 copy-start.6
  29.3 1.0 %copy-done.6 = bf16[128,1152]{1,0:T(8,128)(2,1)S(1)} copy-done((bf16[128,1152]{1,0:T(8,128)(2,1)S(1)}, bf16[128,1152]{1,0:T(8,128)(2,1)}, u32[]{:S(2)}) %copy-start.6) | copy-done | bytes 294936
  30.3 1.1 %pass_on.1 = (bf16[128,1152]{1,0:T(8,128)(2,1)S(1)}, bf16[128,1152]{1,0:T(8,128)(2,1)S(1)}) custom-call(bf16[128,1152]{1,0:T(8,128)(2,1)S(1)} %copy-done.4, bf16[128,1152]{1,0:T(8,128)(2,1)S(1)} %copy-done.6, bf16[128,1152]{1,0:T(8,128)(2,1)S(1)} %collective-permute-done.up_1, bf16[128,1152]{1,0:T(8,128)(2,1)} %collective-permute-done.1.down_1), custom_call_target="tpu_custom_call" | custom-call | tf_op jit(solution)/shard_map/pass_on/pallas_call | solution.py:466
  31.4 0.5 collective-permute-start.5
  31.9 1.0 %collective-permute-start.4 = (bf16[128,1152]{1,0:T(8,128)(2,1)S(1)}, bf16[128,1152]{1,0:T(8,128)(2,1)S(1)}, u32[]{:S(2)}, u32[]{:S(2)}) collective-permute-start(bf16[128,1152]{1,0:T(8,128)(2,1)S(1)} %get-tuple-element.34.after), channel_id=1, source_target_pairs={{0,2},{1,3},{2,4},{3,5},{4,6},{5,7},{6,0},{7,1},{8,10},{9,11},{10,... | collective-permute-start | bytes 884744 | tf_op jit(solution)/shard_map/ppermute | solution.py:474
  33.0 0.0 copy-done.12
  33.0 0.1 convert_reduce_fusion
  33.1 3.4 %copy-done.1 = bf16[4096,1024]{1,0:T(8,128)(2,1)S(1)} copy-done((bf16[4096,1024]{1,0:T(8,128)(2,1)S(1)}, bf16[4096,1024]{1,0:T(8,128)(2,1)}, u32[]{:S(2)}) %copy-start.1) | copy-done | bytes 8388632
  36.5 0.6 fetch_weights.1.after.adapter
  37.0 0.5 collective-permute-done.6.swapped
  37.5 0.0 copy-start.7
  37.5 0.2 add_swapped.1
  37.7 1.4 %collective-permute-start.8 = (bf16[64,1792]{1,0:T(8,128)(2,1)S(1)}, bf16[64,1792]{1,0:T(8,128)(2,1)S(1)}, u32[]{:S(2)}, u32[]{:S(2)}) collective-permute-start(bf16[64,1792]{1,0:T(8,128)(2,1)S(1)} %get-tuple-element.46), channel_id=1, source_target_pairs={{0,2},{1,3},{2,4},{3,5},{4,6},{5,7},{6,0},{7,1},{8,10},{9,11},{10,... | collective-permute-start | bytes 688136 | tf_op jit(solution)/shard_map/ppermute | solution.py:494
  39.1 0.0 collective-permute-done.2.up_near
  39.1 1.7 %collective-permute-start.10 = (bf16[64,1792]{1,0:T(8,128)(2,1)S(1)}, bf16[64,1792]{1,0:T(8,128)(2,1)S(1)}, u32[]{:S(2)}, u32[]{:S(2)}) collective-permute-start(bf16[64,1792]{1,0:T(8,128)(2,1)S(1)} %get-tuple-element.47), channel_id=1, source_target_pairs={{0,6},{1,7},{2,0},{3,1},{4,2},{5,3},{6,4},{7,5},{8,14},{9,15},{10,... | collective-permute-start | bytes 688136 | tf_op jit(solution)/shard_map/ppermute | solution.py:495
  40.8 0.0 collective-permute-done.3.down_near
  40.8 1.4 %collective-permute-start.9 = (bf16[64,1792]{1,0:T(8,128)(2,1)S(1)}, bf16[64,1792]{1,0:T(8,128)(2,1)S(1)}, u32[]{:S(2)}, u32[]{:S(2)}) collective-permute-start(bf16[64,1792]{1,0:T(8,128)(2,1)S(1)} %get-tuple-element.42.after), channel_id=1, source_target_pairs={{0,4},{1,5},{2,6},{3,7},{4,0},{5,1},{6,2},{7,3},{8,12},{9,13},{10,... | collective-permute-start | bytes 688136 | tf_op jit(solution)/shard_map/ppermute | solution.py:493
  42.2 0.0 collective-permute-done.5.down_2
  42.2 0.0 collective-permute-done.4.up_2
  42.2 0.2 fold.1
  42.4 2.7 %collective-permute-start.7 = (bf16[64,2304]{1,0:T(8,128)(2,1)S(1)}, bf16[64,2304]{1,0:T(8,128)(2,1)S(1)}, u32[]{:S(2)}, u32[]{:S(2)}) collective-permute-start(bf16[64,2304]{1,0:T(8,128)(2,1)S(1)} %get-tuple-element.44), channel_id=1, source_target_pairs={{0,1},{1,0},{2,3},{3,2},{4,5},{5,4},{6,7},{7,6},{8,9},{9,8},{10,11... | collective-permute-start | bytes 884744 | tf_op jit(solution)/shard_map/ppermute | solution.py:507
  45.1 0.1 dynamic-slice_bitcast_fusion
  45.2 0.1 convert_divide_fusion.member
  45.3 0.0 collective-permute-done.8.b_1
  45.3 0.0 collective-permute-done.10.b_3
  45.3 5.7 %collective-permute-done.9.b_2 = bf16[64,1792]{1,0:T(8,128)(2,1)S(1)} collective-permute-done((bf16[64,1792]{1,0:T(8,128)(2,1)S(1)}, bf16[64,1792]{1,0:T(8,128)(2,1)S(1)}, u32[]{:S(2)}, u32[]{:S(2)}) %collective-permute-start.9) | collective-permute-done | bytes 229408 | tf_op jit(solution)/shard_map/ppermute | solution.py:493
  51.0 0.0 collective-permute-done.7.a_z
  51.0 0.0 copy-done.7
  51.0 0.0 copy-start.11
  51.0 2.0 %pool_and_project.1 = bf16[8,16,1664]{2,1,0:T(8,128)(2,1)S(1)} custom-call(bf16[64,4096]{1,0:T(8,128)(2,1)S(1)} %constant_dynamic-slice_fusion.rows, bf16[4096,1024]{1,0:T(8,128)(2,1)S(1)} %fetch_weights.1.after.adapter, f32[16,64]{1,0:T(8,128)S(1)} %convert_divide_fusion.member, f32[1,4096]{1,0:T(1,128)S(1)} %bitcast.12, ...), custom_call_target="tpu_custom_call" | custom-call | tf_op jit(solution)/shard_map/pool_and_project/pallas_call | solution.py:515
  53.1 12.8 %all_to_all.10.message = bf16[8,16,1664]{2,1,0:T(8,128)(2,1)S(1)} all-to-all(bf16[8,16,1664]{2,1,0:T(8,128)(2,1)S(1)} %pool_and_project.1), channel_id=1, replica_groups=mesh['dp'=16,'mp'=8] {'mp'}, dimensions={0} | all-to-all | bytes 851968 | tf_op jit(solution)/shard_map/all_to_all | solution.py:527
  65.8 0.1 sum_partials.1
  66.0 12.3 %all_to_all.11 = bf16[8,16,2176]{2,1,0:T(8,128)(2,1)S(1)} all-to-all(bf16[8,16,2176]{2,1,0:T(8,128)(2,1)S(1)} %sum_partials.1), channel_id=1, replica_groups={{0,16,32,48,64,80,96,112},{8,24,40,56,72,88,104,120},{1,17,33,49,65,81,..., dimensions={0} | all-to-all | bytes 1114112 | tf_op jit(solution)/shard_map/all_to_all | solution.py:537
  78.3 5.7 %collective-permute-start.11 = (bf16[128,2176]{1,0:T(8,128)(2,1)S(1)}, bf16[128,2176]{1,0:T(8,128)(2,1)S(1)}, u32[]{:S(2)}, u32[]{:S(2)}) collective-permute-start(bf16[128,2176]{1,0:T(8,128)(2,1)S(1)} %bitcast.10), channel_id=1, source_target_pairs={{0,8},{8,0},{16,24},{24,16},{32,40},{40,32},{48,56},{56,48},{64,72... | collective-permute-start | bytes 1671176 | tf_op jit(solution)/shard_map/ppermute | solution.py:541
  83.9 1.6 %collective-permute-done.11.other = bf16[128,2176]{1,0:T(8,128)(2,1)S(1)} collective-permute-done((bf16[128,2176]{1,0:T(8,128)(2,1)S(1)}, bf16[128,2176]{1,0:T(8,128)(2,1)S(1)}, u32[]{:S(2)}, u32[]{:S(2)}) %collective-permute-start.11) | collective-permute-done | bytes 557088 | tf_op jit(solution)/shard_map/ppermute | solution.py:541
  85.5 0.0 copy-done.11
  85.5 3.0 %loss_and_gradients.1 = (f32[1,1]{1,0:T(1,128)}, f32[32,1024]{1,0:T(8,128)}, f32[2,1024]{1,0:T(2,128)}) custom-call(bf16[128,2176]{1,0:T(8,128)(2,1)S(1)} %bitcast.11, bf16[128,2176]{1,0:T(8,128)(2,1)S(1)} %collective-permute-done.11.other, bf16[2,1024]{1,0:T(2,128)(2,1)S(1)} %copy-done.8, f32[1,1024]{1,0:T(1,128)S(1)} %bitcast.14, f32[1,1024]{1,0:T(1,128)S(1)} %bitcast.16, ...), custom_call_target="tpu_custom_call" | custom-call | tf_op jit(solution)/shard_map/loss_and_gradients/pallas_call | solution.py:544
  (1 shorter events, 0.0 us)
Async XLA Ops:
  0.6 19.3 %copy-start = (bf16[512,4096]{1,0:T(8,128)(2,1)S(1)}, bf16[512,4096]{1,0:T(8,128)(2,1)}, u32[]{:S(2)}) copy-start(bf16[512,4096]{1,0:T(8,128)(2,1)} %w_out.3) | copy-start | bytes 12582916
  0.6 19.3 %copy-start.8 = (bf16[2,1024]{1,0:T(2,128)(2,1)S(1)}, bf16[2,1024]{1,0:T(2,128)(2,1)}, u32[]{:S(2)}) copy-start(bf16[2,1024]{1,0:T(2,128)(2,1)} %features.3) | copy-start | bytes 12292
  0.7 19.3 %copy-start.9 = (f32[1024]{0:T(1024)S(1)}, f32[1024]{0:T(1024)}, u32[]{:S(2)}) copy-start(f32[1024]{0:T(1024)} %param.25) | copy-start | bytes 12292
  0.7 19.3 %copy-start.10 = (f32[1024]{0:T(1024)S(1)}, f32[1024]{0:T(1024)}, u32[]{:S(2)}) copy-start(f32[1024]{0:T(1024)} %param.26) | copy-start | bytes 12292
  12.7 20.3 %copy-start.12 = (s32[1,512]{1,0:T(1,128)S(1)}, s32[1,512]{1,0:T(1,128)}, u32[]{:S(2)}) copy-start(s32[1,512]{1,0:T(1,128)} %seg.1) | copy-start | bytes 6148
  12.7 24.8 %collective-permute-start.6 = (bf16[256,1792]{1,0:T(8,128)(2,1)}, bf16[256,1792]{1,0:T(8,128)(2,1)S(1)}, u32[]{:S(2)}, u32[]{:S(2)}) collective-permute-start(bf16[256,1792]{1,0:T(8,128)(2,1)} %get-tuple-element.41), channel_id=1, source_target_pairs={{0,1},{1,0},{2,3},{3,2},{4,5},{5,4},{6,7},{7,6},{8,9},{9,8},{10,11... | collective-permute-start | bytes 2752520 | tf_op jit(solution)/shard_map/ppermute | solution.py:448
  17.2 11.1 %collective-permute-start = (bf16[128,1152]{1,0:T(8,128)(2,1)}, bf16[128,1152]{1,0:T(8,128)(2,1)S(1)}, u32[]{:S(2)}, u32[]{:S(2)}) collective-permute-start(bf16[128,1152]{1,0:T(8,128)(2,1)} %get-tuple-element.32), channel_id=1, source_target_pairs={{0,2},{1,3},{2,4},{3,5},{4,6},{5,7},{6,0},{7,1},{8,10},{9,11},{10,... | collective-permute-start | bytes 884744 | tf_op jit(solution)/shard_map/ppermute | solution.py:449
  18.5 9.9 %collective-permute-start.1 = (bf16[128,1152]{1,0:T(8,128)(2,1)}, bf16[128,1152]{1,0:T(8,128)(2,1)}, u32[]{:S(2)}, u32[]{:S(2)}) collective-permute-start(bf16[128,1152]{1,0:T(8,128)(2,1)} %get-tuple-element.33), channel_id=1, source_target_pairs={{0,6},{1,7},{2,0},{3,1},{4,2},{5,3},{6,4},{7,5},{8,14},{9,15},{10,... | collective-permute-start | bytes 884744 | tf_op jit(solution)/shard_map/ppermute | solution.py:450
  20.0 1.0 %copy-start.2 = (bf16[512,512]{1,0:T(8,128)(2,1)S(1)}, bf16[512,512]{1,0:T(8,128)(2,1)}, u32[]{:S(2)}) copy-start(bf16[512,512]{1,0:T(8,128)(2,1)} %get-tuple-element.27.ordered) | copy-start | bytes 1572868
  23.1 0.7 copy-start.3
  23.9 0.7 copy-start.5
  24.6 14.5 %collective-permute-start.2 = (bf16[128,1152]{1,0:T(8,128)(2,1)}, bf16[128,1152]{1,0:T(8,128)(2,1)S(1)}, u32[]{:S(2)}, u32[]{:S(2)}) collective-permute-start(bf16[128,1152]{1,0:T(8,128)(2,1)} %get-tuple-element.37), channel_id=1, source_target_pairs={{0,2},{1,3},{2,4},{3,5},{4,6},{5,7},{6,0},{7,1},{8,10},{9,11},{10,... | collective-permute-start | bytes 884744 | tf_op jit(solution)/shard_map/ppermute | solution.py:462
  24.6 16.2 %collective-permute-start.3 = (bf16[128,1152]{1,0:T(8,128)(2,1)}, bf16[128,1152]{1,0:T(8,128)(2,1)S(1)}, u32[]{:S(2)}, u32[]{:S(2)}) collective-permute-start(bf16[128,1152]{1,0:T(8,128)(2,1)} %get-tuple-element.38), channel_id=1, source_target_pairs={{0,6},{1,7},{2,0},{3,1},{4,2},{5,3},{6,4},{7,5},{8,14},{9,15},{10,... | collective-permute-start | bytes 884744 | tf_op jit(solution)/shard_map/ppermute | solution.py:463
  28.4 1.0 %copy-start.4 = (bf16[128,1152]{1,0:T(8,128)(2,1)S(1)}, bf16[128,1152]{1,0:T(8,128)(2,1)}, u32[]{:S(2)}) copy-start(bf16[128,1152]{1,0:T(8,128)(2,1)} %copy-done.3) | copy-start | bytes 884740
  29.3 1.0 %copy-start.6 = (bf16[128,1152]{1,0:T(8,128)(2,1)S(1)}, bf16[128,1152]{1,0:T(8,128)(2,1)}, u32[]{:S(2)}) copy-start(bf16[128,1152]{1,0:T(8,128)(2,1)} %copy-done.5) | copy-start | bytes 884740
  31.4 10.7 %collective-permute-start.5 = (bf16[128,1152]{1,0:T(8,128)(2,1)S(1)}, bf16[128,1152]{1,0:T(8,128)(2,1)S(1)}, u32[]{:S(2)}, u32[]{:S(2)}) collective-permute-start(bf16[128,1152]{1,0:T(8,128)(2,1)S(1)} %get-tuple-element.39), channel_id=1, source_target_pairs={{0,6},{1,7},{2,0},{3,1},{4,2},{5,3},{6,4},{7,5},{8,14},{9,15},{10,... | collective-permute-start | bytes 884744 | tf_op jit(solution)/shard_map/ppermute | solution.py:475
  31.9 10.3 %collective-permute-start.4 = (bf16[128,1152]{1,0:T(8,128)(2,1)S(1)}, bf16[128,1152]{1,0:T(8,128)(2,1)S(1)}, u32[]{:S(2)}, u32[]{:S(2)}) collective-permute-start(bf16[128,1152]{1,0:T(8,128)(2,1)S(1)} %get-tuple-element.34.after), channel_id=1, source_target_pairs={{0,2},{1,3},{2,4},{3,5},{4,6},{5,7},{6,0},{7,1},{8,10},{9,11},{10,... | collective-permute-start | bytes 884744 | tf_op jit(solution)/shard_map/ppermute | solution.py:474
  33.1 3.4 %copy-start.1 = (bf16[4096,1024]{1,0:T(8,128)(2,1)S(1)}, bf16[4096,1024]{1,0:T(8,128)(2,1)}, u32[]{:S(2)}) copy-start(bf16[4096,1024]{1,0:T(8,128)(2,1)} %adapter.1) | copy-start | bytes 25165828
  37.5 13.5 %copy-start.7 = (f32[4096]{0:T(1024)S(1)}, f32[4096]{0:T(1024)}, u32[]{:S(2)}) copy-start(f32[4096]{0:T(1024)} %param.22) | copy-start | bytes 49156
  37.7 7.6 %collective-permute-start.8 = (bf16[64,1792]{1,0:T(8,128)(2,1)S(1)}, bf16[64,1792]{1,0:T(8,128)(2,1)S(1)}, u32[]{:S(2)}, u32[]{:S(2)}) collective-permute-start(bf16[64,1792]{1,0:T(8,128)(2,1)S(1)} %get-tuple-element.46), channel_id=1, source_target_pairs={{0,2},{1,3},{2,4},{3,5},{4,6},{5,7},{6,0},{7,1},{8,10},{9,11},{10,... | collective-permute-start | bytes 688136 | tf_op jit(solution)/shard_map/ppermute | solution.py:494
  39.1 6.2 %collective-permute-start.10 = (bf16[64,1792]{1,0:T(8,128)(2,1)S(1)}, bf16[64,1792]{1,0:T(8,128)(2,1)S(1)}, u32[]{:S(2)}, u32[]{:S(2)}) collective-permute-start(bf16[64,1792]{1,0:T(8,128)(2,1)S(1)} %get-tuple-element.47), channel_id=1, source_target_pairs={{0,6},{1,7},{2,0},{3,1},{4,2},{5,3},{6,4},{7,5},{8,14},{9,15},{10,... | collective-permute-start | bytes 688136 | tf_op jit(solution)/shard_map/ppermute | solution.py:495
  40.8 10.2 %collective-permute-start.9 = (bf16[64,1792]{1,0:T(8,128)(2,1)S(1)}, bf16[64,1792]{1,0:T(8,128)(2,1)S(1)}, u32[]{:S(2)}, u32[]{:S(2)}) collective-permute-start(bf16[64,1792]{1,0:T(8,128)(2,1)S(1)} %get-tuple-element.42.after), channel_id=1, source_target_pairs={{0,4},{1,5},{2,6},{3,7},{4,0},{5,1},{6,2},{7,3},{8,12},{9,13},{10,... | collective-permute-start | bytes 688136 | tf_op jit(solution)/shard_map/ppermute | solution.py:493
  42.4 8.6 %collective-permute-start.7 = (bf16[64,2304]{1,0:T(8,128)(2,1)S(1)}, bf16[64,2304]{1,0:T(8,128)(2,1)S(1)}, u32[]{:S(2)}, u32[]{:S(2)}) collective-permute-start(bf16[64,2304]{1,0:T(8,128)(2,1)S(1)} %get-tuple-element.44), channel_id=1, source_target_pairs={{0,1},{1,0},{2,3},{3,2},{4,5},{5,4},{6,7},{7,6},{8,9},{9,8},{10,11... | collective-permute-start | bytes 884744 | tf_op jit(solution)/shard_map/ppermute | solution.py:507
  51.0 34.5 %copy-start.11 = (s32[256]{0:T(256)S(1)}, s32[256]{0:T(256)}, u32[]{:S(2)}) copy-start(s32[256]{0:T(256)} %param.27) | copy-start | bytes 3076
  78.3 7.3 %collective-permute-start.11 = (bf16[128,2176]{1,0:T(8,128)(2,1)S(1)}, bf16[128,2176]{1,0:T(8,128)(2,1)S(1)}, u32[]{:S(2)}, u32[]{:S(2)}) collective-permute-start(bf16[128,2176]{1,0:T(8,128)(2,1)S(1)} %bitcast.10), channel_id=1, source_target_pairs={{0,8},{8,0},{16,24},{24,16},{32,40},{40,32},{48,56},{56,48},{64,72... | collective-permute-start | bytes 1671176 | tf_op jit(solution)/shard_map/ppermute | solution.py:541

commit v2 on v0

--- a/solution.py
+++ b/solution.py
@@ -41,7 +41,7 @@
 ):
     length, width = hidden.shape
     q_local = w_query.shape[1] // HD
-    parts = 4
+    parts = 8
     span = width // parts
     q_cols = w_query.shape[1]
     kv_cols = w_key.shape[1]
@@ -437,7 +437,7 @@
             pltpu.VMEM((length, q_cols), BF16),
             pltpu.VMEM((2 * small, cut), BF16),
             pltpu.VMEM(late.shape, BF16),
-            pltpu.SemaphoreType.DMA((5, 4)),
+            pltpu.SemaphoreType.DMA((9, 4)),
             pltpu.SemaphoreType.DMA((4,)),
         ],
         compiler_params=pltpu.CompilerParams(vmem_limit_bytes=56 * 1024 * 1024),

time: 89.7 us -> 89.6 us (level)
  transfers between devices with their start and end apart: 12 -> 12, of which waited for: 3 -> 3; matrix products, arithmetic and copies ran while one was open for 2% -> 2% of each run, Pallas kernels for 4% -> 5%
where the time goes in v2:
time: 89.6 us; the launch traced here: 89.2 us
  blocking collectives  25.1 us (28%)
  starting transfers between devices  24.3 us (27%)
  Pallas kernels  21.8 us (24%)
  local copies, waits for them, and re-layouts  8.98 us (10%)
  waiting for transfers between devices  8.03 us (9%)
    all_to_all x1, blocking collectives, on_device(): message = lax.all_to_all(message, 'mp', 0, 0, tiled=True)  12.8 us
    all_to_all x1, blocking collectives, on_device(): lax.all_to_all(second, 'dp', 0, 0, tiled=True, axis_index_groups=[[2 * ch...  12.3 us
    pallas_call x1, Pallas kernels, on_device(): pl.pallas_call(text_kernel, out_shape=[late, one, one, jax.ShapeDtypeStru...  11.7 us
    unnamed x26, local copies, waits for them, and re-layouts  7.83 us
    ppermute x1, waiting for transfers between devices, on_device(): q_2 = lax.ppermute(blocks[2], 'mp', y_shift(2))  5.73 us
    ppermute x1, starting transfers between devices, on_device(): other = lax.ppermute(second, 'dp', [(d, d ^ 1) for d in range(seqs)])  5.69 us
    ppermute x1, starting transfers between devices, on_device(): swapped = lax.ppermute(send, 'mp', Z_SWAP)  4.51 us
    pallas_call x1, Pallas kernels, on_device(): pl.pallas_call(loss_kernel, out_shape=[jax.ShapeDtypeStruct((1, 1), F32),...  3.94 us
  transfers between devices with their start and end apart: 12, of which 3 were waited for; matrix products, arithmetic and copies ran while one was open for 2% of the time, Pallas kernels for 5%

profile of v2, /device:TPU:1, one launch (start us, length us, event | category | flops | bytes accessed | tf_op | source)
XLA Modules:
  0.0 89.2 jit_solution(9219119326372940865)
XLA Ops:
  0.6 0.0 copy-start
  0.6 11.7 %text_tower.1 = (bf16[256,1792]{1,0:T(8,128)(2,1)}, bf16[128,1152]{1,0:T(8,128)(2,1)}, bf16[128,1152]{1,0:T(8,128)(2,1)}, bf16[512,512]{1,0:T(8,128)(2,1)}) custom-call(bf16[512,4096]{1,0:T(8,128)(2,1)} %hidden.1, bf16[4096,512]{1,0:T(8,128)(2,1)} %w_query.1, bf16[4096,128]{1,0:T(8,128)(2,1)} %w_key.1, bf16[4096,128]{1,0:T(8,128)(2,1)} %w_value.1, ...), custom_call_target="tpu_custom_call" | custom-call | tf_op jit(solution)/shard_map/text_tower/pallas_call | solution.py:422
  12.3 0.0 copy-start.12
  12.4 4.5 %collective-permute-start.6 = (bf16[256,1792]{1,0:T(8,128)(2,1)}, bf16[256,1792]{1,0:T(8,128)(2,1)S(1)}, u32[]{:S(2)}, u32[]{:S(2)}) collective-permute-start(bf16[256,1792]{1,0:T(8,128)(2,1)} %get-tuple-element.39), channel_id=1, source_target_pairs={{0,1},{1,0},{2,3},{3,2},{4,5},{5,4},{6,7},{7,6},{8,9},{9,8},{10,11... | collective-permute-start | bytes 2752520 | tf_op jit(solution)/shard_map/ppermute | solution.py:449
  16.9 1.3 %collective-permute-start = (bf16[128,1152]{1,0:T(8,128)(2,1)}, bf16[128,1152]{1,0:T(8,128)(2,1)S(1)}, u32[]{:S(2)}, u32[]{:S(2)}) collective-permute-start(bf16[128,1152]{1,0:T(8,128)(2,1)} %get-tuple-element.31), channel_id=1, source_target_pairs={{0,2},{1,3},{2,4},{3,5},{4,6},{5,7},{6,0},{7,1},{8,10},{9,11},{10,... | collective-permute-start | bytes 884744 | tf_op jit(solution)/shard_map/ppermute | solution.py:450
  18.2 1.4 %collective-permute-start.1 = (bf16[128,1152]{1,0:T(8,128)(2,1)}, bf16[128,1152]{1,0:T(8,128)(2,1)}, u32[]{:S(2)}, u32[]{:S(2)}) collective-permute-start(bf16[128,1152]{1,0:T(8,128)(2,1)} %get-tuple-element.32), channel_id=1, source_target_pairs={{0,6},{1,7},{2,0},{3,1},{4,2},{5,3},{6,4},{7,5},{8,14},{9,15},{10,... | collective-permute-start | bytes 884744 | tf_op jit(solution)/shard_map/ppermute | solution.py:451
  19.6 0.0 copy-done
  19.6 0.0 copy-start.2
  19.6 1.0 %copy-done.2 = bf16[512,512]{1,0:T(8,128)(2,1)S(1)} copy-done((bf16[512,512]{1,0:T(8,128)(2,1)S(1)}, bf16[512,512]{1,0:T(8,128)(2,1)}, u32[]{:S(2)}) %copy-start.2) | copy-done | bytes 524312
  20.6 1.9 %other_terms.1 = (bf16[128,1152]{1,0:T(8,128)(2,1)}, bf16[128,1152]{1,0:T(8,128)(2,1)}, bf16[128,1152]{1,0:T(8,128)(2,1)S(1)}, bf16[128,1152]{1,0:T(8,128)(2,1)S...) custom-call(bf16[512,512]{1,0:T(8,128)(2,1)S(1)} %copy-done.2, bf16[512,4096]{1,0:T(8,128)(2,1)S(1)} %copy-done), custom_call_target="tpu_custom_call" | custom-call | flops 1073741824 | bytes 8388608 | tf_op jit(solution)/shard_map/other_terms/pallas_call | solution.py:452
  22.6 0.0 copy-start.3
  22.6 0.7 copy-done.3
  23.3 0.0 copy-start.5
  23.3 0.7 copy-done.5
  24.0 0.0 collective-permute-start.2
  24.0 2.7 %collective-permute-start.3 = (bf16[128,1152]{1,0:T(8,128)(2,1)}, bf16[128,1152]{1,0:T(8,128)(2,1)S(1)}, u32[]{:S(2)}, u32[]{:S(2)}) collective-permute-start(bf16[128,1152]{1,0:T(8,128)(2,1)} %get-tuple-element.36), channel_id=1, source_target_pairs={{0,6},{1,7},{2,0},{3,1},{4,2},{5,3},{6,4},{7,5},{8,14},{9,15},{10,... | collective-permute-start | bytes 884744 | tf_op jit(solution)/shard_map/ppermute | solution.py:464
  26.7 1.1 %constant_dynamic-slice_fusion.rows = bf16[64,4096]{1,0:T(8,128)(2,1)S(1)} fusion(bf16[512,4096]{1,0:T(8,128)(2,1)} %hidden.1, s32[]{:T(128)S(6)} %select_n.4), kind=kLoop, calls=%fused_computation.5 | loop fusion | bytes 1048580 | tf_op jit(solution)/shard_map/dynamic_slice | solution.py:465
  27.8 0.0 collective-permute-done.up_1
  27.8 0.0 collective-permute-done.1.down_1
  27.8 0.0 copy-start.4
  27.8 1.0 %copy-done.4 = bf16[128,1152]{1,0:T(8,128)(2,1)S(1)} copy-done((bf16[128,1152]{1,0:T(8,128)(2,1)S(1)}, bf16[128,1152]{1,0:T(8,128)(2,1)}, u32[]{:S(2)}) %copy-start.4) | copy-done | bytes 294936
  28.8 0.0 copy-start.6
  28.8 1.0 %copy-done.6 = bf16[128,1152]{1,0:T(8,128)(2,1)S(1)} copy-done((bf16[128,1152]{1,0:T(8,128)(2,1)S(1)}, bf16[128,1152]{1,0:T(8,128)(2,1)}, u32[]{:S(2)}) %copy-start.6) | copy-done | bytes 294936
  29.7 1.1 %pass_on.1 = (bf16[128,1152]{1,0:T(8,128)(2,1)S(1)}, bf16[128,1152]{1,0:T(8,128)(2,1)S(1)}) custom-call(bf16[128,1152]{1,0:T(8,128)(2,1)S(1)} %copy-done.4, bf16[128,1152]{1,0:T(8,128)(2,1)S(1)} %copy-done.6, bf16[128,1152]{1,0:T(8,128)(2,1)S(1)} %collective-permute-done.up_1, bf16[128,1152]{1,0:T(8,128)(2,1)} %collective-permute-done.1.down_1), custom_call_target="tpu_custom_call" | custom-call | tf_op jit(solution)/shard_map/pass_on/pallas_call | solution.py:467
  30.8 0.7 collective-permute-start.5
  31.5 0.8 collective-permute-start.4
  32.4 0.0 copy-done.12
  32.4 0.1 convert_reduce_fusion
  32.5 0.0 copy-start.1
  32.5 3.4 %copy-done.1 = bf16[4096,1024]{1,0:T(8,128)(2,1)S(1)} copy-done((bf16[4096,1024]{1,0:T(8,128)(2,1)S(1)}, bf16[4096,1024]{1,0:T(8,128)(2,1)}, u32[]{:S(2)}) %copy-start.1) | copy-done | bytes 8388632
  35.9 0.6 fetch_weights.1.after.adapter
  36.4 0.7 collective-permute-done.6.swapped
  37.1 0.0 copy-start.7
  37.2 0.2 add_swapped.1
  37.4 1.4 %collective-permute-start.8 = (bf16[64,1792]{1,0:T(8,128)(2,1)S(1)}, bf16[64,1792]{1,0:T(8,128)(2,1)S(1)}, u32[]{:S(2)}, u32[]{:S(2)}) collective-permute-start(bf16[64,1792]{1,0:T(8,128)(2,1)S(1)} %get-tuple-element.44), channel_id=1, source_target_pairs={{0,2},{1,3},{2,4},{3,5},{4,6},{5,7},{6,0},{7,1},{8,10},{9,11},{10,... | collective-permute-start | bytes 688136 | tf_op jit(solution)/shard_map/ppermute | solution.py:495
  38.7 0.0 collective-permute-done.2.up_near
  38.7 1.7 %collective-permute-start.10 = (bf16[64,1792]{1,0:T(8,128)(2,1)S(1)}, bf16[64,1792]{1,0:T(8,128)(2,1)S(1)}, u32[]{:S(2)}, u32[]{:S(2)}) collective-permute-start(bf16[64,1792]{1,0:T(8,128)(2,1)S(1)} %get-tuple-element.45), channel_id=1, source_target_pairs={{0,6},{1,7},{2,0},{3,1},{4,2},{5,3},{6,4},{7,5},{8,14},{9,15},{10,... | collective-permute-start | bytes 688136 | tf_op jit(solution)/shard_map/ppermute | solution.py:496
  40.4 0.0 collective-permute-done.3.down_near
  40.4 1.4 %collective-permute-start.9 = (bf16[64,1792]{1,0:T(8,128)(2,1)S(1)}, bf16[64,1792]{1,0:T(8,128)(2,1)S(1)}, u32[]{:S(2)}, u32[]{:S(2)}) collective-permute-start(bf16[64,1792]{1,0:T(8,128)(2,1)S(1)} %get-tuple-element.40.after), channel_id=1, source_target_pairs={{0,4},{1,5},{2,6},{3,7},{4,0},{5,1},{6,2},{7,3},{8,12},{9,13},{10,... | collective-permute-start | bytes 688136 | tf_op jit(solution)/shard_map/ppermute | solution.py:494
  41.8 0.0 collective-permute-done.5.down_2
  41.8 0.0 collective-permute-done.4.up_2
  41.8 0.2 fold.1
  42.0 2.7 %collective-permute-start.7 = (bf16[64,2304]{1,0:T(8,128)(2,1)S(1)}, bf16[64,2304]{1,0:T(8,128)(2,1)S(1)}, u32[]{:S(2)}, u32[]{:S(2)}) collective-permute-start(bf16[64,2304]{1,0:T(8,128)(2,1)S(1)} %get-tuple-element.42), channel_id=1, source_target_pairs={{0,1},{1,0},{2,3},{3,2},{4,5},{5,4},{6,7},{7,6},{8,9},{9,8},{10,11... | collective-permute-start | bytes 884744 | tf_op jit(solution)/shard_map/ppermute | solution.py:508
  44.8 0.1 dynamic-slice_bitcast_fusion
  44.8 0.1 convert_divide_fusion.member
  44.9 0.0 collective-permute-done.8.b_1
  44.9 0.0 collective-permute-done.10.b_3
  44.9 5.7 %collective-permute-done.9.b_2 = bf16[64,1792]{1,0:T(8,128)(2,1)S(1)} collective-permute-done((bf16[64,1792]{1,0:T(8,128)(2,1)S(1)}, bf16[64,1792]{1,0:T(8,128)(2,1)S(1)}, u32[]{:S(2)}, u32[]{:S(2)}) %collective-permute-start.9) | collective-permute-done | bytes 229408 | tf_op jit(solution)/shard_map/ppermute | solution.py:494
  50.7 0.0 collective-permute-done.7.a_z
  50.7 0.0 copy-done.7
  50.7 0.0 copy-done.8
  50.7 0.0 copy-start.9
  50.7 0.0 copy-start.10
  50.7 0.0 copy-start.11
  50.7 2.0 %pool_and_project.1 = bf16[8,16,1664]{2,1,0:T(8,128)(2,1)S(1)} custom-call(bf16[64,4096]{1,0:T(8,128)(2,1)S(1)} %constant_dynamic-slice_fusion.rows, bf16[4096,1024]{1,0:T(8,128)(2,1)S(1)} %fetch_weights.1.after.adapter, f32[16,64]{1,0:T(8,128)S(1)} %convert_divide_fusion.member, f32[1,4096]{1,0:T(1,128)S(1)} %bitcast.12, bf16[2,1024]{1,0:T(2,128)(2,1)S(1)} %copy-done.8, ...), custom_call_target="tpu_custom_call" | custom-call | tf_op jit(solution)/shard_map/pool_and_project/pallas_call | solution.py:516
  52.7 12.8 %all_to_all.10.message = bf16[8,16,1664]{2,1,0:T(8,128)(2,1)S(1)} all-to-all(bf16[8,16,1664]{2,1,0:T(8,128)(2,1)S(1)} %pool_and_project.1), channel_id=1, replica_groups=mesh['dp'=16,'mp'=8] {'mp'}, dimensions={0} | all-to-all | bytes 851968 | tf_op jit(solution)/shard_map/all_to_all | solution.py:528
  65.5 0.1 sum_partials.1
  65.6 12.3 %all_to_all.11 = bf16[8,16,2176]{2,1,0:T(8,128)(2,1)S(1)} all-to-all(bf16[8,16,2176]{2,1,0:T(8,128)(2,1)S(1)} %sum_partials.1), channel_id=1, replica_groups={{0,16,32,48,64,80,96,112},{8,24,40,56,72,88,104,120},{1,17,33,49,65,81,..., dimensions={0} | all-to-all | bytes 1114112 | tf_op jit(solution)/shard_map/all_to_all | solution.py:538
  77.9 5.7 %collective-permute-start.11 = (bf16[128,2176]{1,0:T(8,128)(2,1)S(1)}, bf16[128,2176]{1,0:T(8,128)(2,1)S(1)}, u32[]{:S(2)}, u32[]{:S(2)}) collective-permute-start(bf16[128,2176]{1,0:T(8,128)(2,1)S(1)} %bitcast.10), channel_id=1, source_target_pairs={{0,8},{8,0},{16,24},{24,16},{32,40},{40,32},{48,56},{56,48},{64,72... | collective-permute-start | bytes 1671176 | tf_op jit(solution)/shard_map/ppermute | solution.py:542
  83.6 1.6 %collective-permute-done.11.other = bf16[128,2176]{1,0:T(8,128)(2,1)S(1)} collective-permute-done((bf16[128,2176]{1,0:T(8,128)(2,1)S(1)}, bf16[128,2176]{1,0:T(8,128)(2,1)S(1)}, u32[]{:S(2)}, u32[]{:S(2)}) %collective-permute-start.11) | collective-permute-done | bytes 557088 | tf_op jit(solution)/shard_map/ppermute | solution.py:542
  85.2 0.0 copy-done.9
  85.2 0.0 copy-done.10
  85.2 0.0 copy-done.11
  85.2 3.9 %loss_and_gradients.1 = (f32[1,1]{1,0:T(1,128)}, f32[32,1024]{1,0:T(8,128)}, f32[2,1024]{1,0:T(2,128)}) custom-call(bf16[128,2176]{1,0:T(8,128)(2,1)S(1)} %bitcast.11, bf16[128,2176]{1,0:T(8,128)(2,1)S(1)} %collective-permute-done.11.other, bf16[2,1024]{1,0:T(2,128)(2,1)S(1)} %copy-done.8, f32[1,1024]{1,0:T(1,128)S(1)} %bitcast.13, f32[1,1024]{1,0:T(1,128)S(1)} %bitcast.14, ...), custom_call_target="tpu_custom_call" | custom-call | tf_op jit(solution)/shard_map/loss_and_gradients/pallas_call | solution.py:545
  (1 shorter events, 0.0 us)
Async XLA Ops:
  0.6 19.0 %copy-start = (bf16[512,4096]{1,0:T(8,128)(2,1)S(1)}, bf16[512,4096]{1,0:T(8,128)(2,1)}, u32[]{:S(2)}) copy-start(bf16[512,4096]{1,0:T(8,128)(2,1)} %w_out.3) | copy-start | bytes 12582916
  12.3 20.0 %copy-start.12 = (s32[1,512]{1,0:T(1,128)S(1)}, s32[1,512]{1,0:T(1,128)}, u32[]{:S(2)}) copy-start(s32[1,512]{1,0:T(1,128)} %seg.1) | copy-start | bytes 6148
  12.4 24.8 %collective-permute-start.6 = (bf16[256,1792]{1,0:T(8,128)(2,1)}, bf16[256,1792]{1,0:T(8,128)(2,1)S(1)}, u32[]{:S(2)}, u32[]{:S(2)}) collective-permute-start(bf16[256,1792]{1,0:T(8,128)(2,1)} %get-tuple-element.39), channel_id=1, source_target_pairs={{0,1},{1,0},{2,3},{3,2},{4,5},{5,4},{6,7},{7,6},{8,9},{9,8},{10,11... | collective-permute-start | bytes 2752520 | tf_op jit(solution)/shard_map/ppermute | solution.py:449
  16.9 10.9 %collective-permute-start = (bf16[128,1152]{1,0:T(8,128)(2,1)}, bf16[128,1152]{1,0:T(8,128)(2,1)S(1)}, u32[]{:S(2)}, u32[]{:S(2)}) collective-permute-start(bf16[128,1152]{1,0:T(8,128)(2,1)} %get-tuple-element.31), channel_id=1, source_target_pairs={{0,2},{1,3},{2,4},{3,5},{4,6},{5,7},{6,0},{7,1},{8,10},{9,11},{10,... | collective-permute-start | bytes 884744 | tf_op jit(solution)/shard_map/ppermute | solution.py:450
  18.2 9.6 %collective-permute-start.1 = (bf16[128,1152]{1,0:T(8,128)(2,1)}, bf16[128,1152]{1,0:T(8,128)(2,1)}, u32[]{:S(2)}, u32[]{:S(2)}) collective-permute-start(bf16[128,1152]{1,0:T(8,128)(2,1)} %get-tuple-element.32), channel_id=1, source_target_pairs={{0,6},{1,7},{2,0},{3,1},{4,2},{5,3},{6,4},{7,5},{8,14},{9,15},{10,... | collective-permute-start | bytes 884744 | tf_op jit(solution)/shard_map/ppermute | solution.py:451
  19.6 1.0 %copy-start.2 = (bf16[512,512]{1,0:T(8,128)(2,1)S(1)}, bf16[512,512]{1,0:T(8,128)(2,1)}, u32[]{:S(2)}) copy-start(bf16[512,512]{1,0:T(8,128)(2,1)} %get-tuple-element.26.ordered) | copy-start | bytes 1572868
  22.6 0.7 copy-start.3
  23.3 0.7 copy-start.5
  24.0 14.7 %collective-permute-start.2 = (bf16[128,1152]{1,0:T(8,128)(2,1)}, bf16[128,1152]{1,0:T(8,128)(2,1)S(1)}, u32[]{:S(2)}, u32[]{:S(2)}) collective-permute-start(bf16[128,1152]{1,0:T(8,128)(2,1)} %get-tuple-element.35), channel_id=1, source_target_pairs={{0,2},{1,3},{2,4},{3,5},{4,6},{5,7},{6,0},{7,1},{8,10},{9,11},{10,... | collective-permute-start | bytes 884744 | tf_op jit(solution)/shard_map/ppermute | solution.py:463
  24.0 16.4 %collective-permute-start.3 = (bf16[128,1152]{1,0:T(8,128)(2,1)}, bf16[128,1152]{1,0:T(8,128)(2,1)S(1)}, u32[]{:S(2)}, u32[]{:S(2)}) collective-permute-start(bf16[128,1152]{1,0:T(8,128)(2,1)} %get-tuple-element.36), channel_id=1, source_target_pairs={{0,6},{1,7},{2,0},{3,1},{4,2},{5,3},{6,4},{7,5},{8,14},{9,15},{10,... | collective-permute-start | bytes 884744 | tf_op jit(solution)/shard_map/ppermute | solution.py:464
  27.8 1.0 %copy-start.4 = (bf16[128,1152]{1,0:T(8,128)(2,1)S(1)}, bf16[128,1152]{1,0:T(8,128)(2,1)}, u32[]{:S(2)}) copy-start(bf16[128,1152]{1,0:T(8,128)(2,1)} %copy-done.3) | copy-start | bytes 884740
  28.8 1.0 %copy-start.6 = (bf16[128,1152]{1,0:T(8,128)(2,1)S(1)}, bf16[128,1152]{1,0:T(8,128)(2,1)}, u32[]{:S(2)}) copy-start(bf16[128,1152]{1,0:T(8,128)(2,1)} %copy-done.5) | copy-start | bytes 884740
  30.8 11.0 %collective-permute-start.5 = (bf16[128,1152]{1,0:T(8,128)(2,1)S(1)}, bf16[128,1152]{1,0:T(8,128)(2,1)S(1)}, u32[]{:S(2)}, u32[]{:S(2)}) collective-permute-start(bf16[128,1152]{1,0:T(8,128)(2,1)S(1)} %get-tuple-element.37), channel_id=1, source_target_pairs={{0,6},{1,7},{2,0},{3,1},{4,2},{5,3},{6,4},{7,5},{8,14},{9,15},{10,... | collective-permute-start | bytes 884744 | tf_op jit(solution)/shard_map/ppermute | solution.py:476
  31.5 10.3 %collective-permute-start.4 = (bf16[128,1152]{1,0:T(8,128)(2,1)S(1)}, bf16[128,1152]{1,0:T(8,128)(2,1)S(1)}, u32[]{:S(2)}, u32[]{:S(2)}) collective-permute-start(bf16[128,1152]{1,0:T(8,128)(2,1)S(1)} %get-tuple-element.33.after), channel_id=1, source_target_pairs={{0,2},{1,3},{2,4},{3,5},{4,6},{5,7},{6,0},{7,1},{8,10},{9,11},{10,... | collective-permute-start | bytes 884744 | tf_op jit(solution)/shard_map/ppermute | solution.py:475
  32.5 3.4 %copy-start.1 = (bf16[4096,1024]{1,0:T(8,128)(2,1)S(1)}, bf16[4096,1024]{1,0:T(8,128)(2,1)}, u32[]{:S(2)}) copy-start(bf16[4096,1024]{1,0:T(8,128)(2,1)} %adapter.1) | copy-start | bytes 25165828
  37.1 13.5 %copy-start.7 = (f32[4096]{0:T(1024)S(1)}, f32[4096]{0:T(1024)}, u32[]{:S(2)}) copy-start(f32[4096]{0:T(1024)} %param.22) | copy-start | bytes 49156
  37.1 13.5 %copy-start.8 = (bf16[2,1024]{1,0:T(2,128)(2,1)S(1)}, bf16[2,1024]{1,0:T(2,128)(2,1)}, u32[]{:S(2)}) copy-start(bf16[2,1024]{1,0:T(2,128)(2,1)} %features.3) | copy-start | bytes 12292
  37.4 7.6 %collective-permute-start.8 = (bf16[64,1792]{1,0:T(8,128)(2,1)S(1)}, bf16[64,1792]{1,0:T(8,128)(2,1)S(1)}, u32[]{:S(2)}, u32[]{:S(2)}) collective-permute-start(bf16[64,1792]{1,0:T(8,128)(2,1)S(1)} %get-tuple-element.44), channel_id=1, source_target_pairs={{0,2},{1,3},{2,4},{3,5},{4,6},{5,7},{6,0},{7,1},{8,10},{9,11},{10,... | collective-permute-start | bytes 688136 | tf_op jit(solution)/shard_map/ppermute | solution.py:495
  38.7 6.2 %collective-permute-start.10 = (bf16[64,1792]{1,0:T(8,128)(2,1)S(1)}, bf16[64,1792]{1,0:T(8,128)(2,1)S(1)}, u32[]{:S(2)}, u32[]{:S(2)}) collective-permute-start(bf16[64,1792]{1,0:T(8,128)(2,1)S(1)} %get-tuple-element.45), channel_id=1, source_target_pairs={{0,6},{1,7},{2,0},{3,1},{4,2},{5,3},{6,4},{7,5},{8,14},{9,15},{10,... | collective-permute-start | bytes 688136 | tf_op jit(solution)/shard_map/ppermute | solution.py:496
  40.4 10.2 %collective-permute-start.9 = (bf16[64,1792]{1,0:T(8,128)(2,1)S(1)}, bf16[64,1792]{1,0:T(8,128)(2,1)S(1)}, u32[]{:S(2)}, u32[]{:S(2)}) collective-permute-start(bf16[64,1792]{1,0:T(8,128)(2,1)S(1)} %get-tuple-element.40.after), channel_id=1, source_target_pairs={{0,4},{1,5},{2,6},{3,7},{4,0},{5,1},{6,2},{7,3},{8,12},{9,13},{10,... | collective-permute-start | bytes 688136 | tf_op jit(solution)/shard_map/ppermute | solution.py:494
  42.0 8.6 %collective-permute-start.7 = (bf16[64,2304]{1,0:T(8,128)(2,1)S(1)}, bf16[64,2304]{1,0:T(8,128)(2,1)S(1)}, u32[]{:S(2)}, u32[]{:S(2)}) collective-permute-start(bf16[64,2304]{1,0:T(8,128)(2,1)S(1)} %get-tuple-element.42), channel_id=1, source_target_pairs={{0,1},{1,0},{2,3},{3,2},{4,5},{5,4},{6,7},{7,6},{8,9},{9,8},{10,11... | collective-permute-start | bytes 884744 | tf_op jit(solution)/shard_map/ppermute | solution.py:508
  50.7 34.5 %copy-start.9 = (f32[1024]{0:T(1024)S(1)}, f32[1024]{0:T(1024)}, u32[]{:S(2)}) copy-start(f32[1024]{0:T(1024)} %param.25) | copy-start | bytes 12292
  50.7 34.5 %copy-start.10 = (f32[1024]{0:T(1024)S(1)}, f32[1024]{0:T(1024)}, u32[]{:S(2)}) copy-start(f32[1024]{0:T(1024)} %param.26) | copy-start | bytes 12292
  50.7 34.5 %copy-start.11 = (s32[256]{0:T(256)S(1)}, s32[256]{0:T(256)}, u32[]{:S(2)}) copy-start(s32[256]{0:T(256)} %param.27) | copy-start | bytes 3076
  77.9 7.3 %collective-permute-start.11 = (bf16[128,2176]{1,0:T(8,128)(2,1)S(1)}, bf16[128,2176]{1,0:T(8,128)(2,1)S(1)}, u32[]{:S(2)}, u32[]{:S(2)}) collective-permute-start(bf16[128,2176]{1,0:T(8,128)(2,1)S(1)} %bitcast.10), channel_id=1, source_target_pairs={{0,8},{8,0},{16,24},{24,16},{32,40},{40,32},{48,56},{56,48},{64,72... | collective-permute-start | bytes 1671176 | tf_op jit(solution)/shard_map/ppermute | solution.py:542
